TPU v7x, 32 devices: a whole 2x2x4 slice. The times are simulated.
32 devices in a mesh: groups: 2 (over y), dom: 4 (over z), rep: 4 (over x, core).
Axes of the slice: x: 2, y: 2, z: 4, core: 2. Of those that a mesh axis runs over, the one named last changes fastest.
Arguments:
- grad_out: bfloat16 [8192, 512], P(('groups', 'dom')), parts along dimension 0, may hold values from -6 to 6
- source_features: bfloat16 [16384, 512], P(('groups', 'dom')), parts along dimension 0, may hold values from -6 to 6
- rel_weight: bfloat16 [8, 512, 512], P('rep'), may hold values from -0.25 to 0.25
- self_weight: bfloat16 [512, 512], P('rep'), may hold values from -0.25 to 0.25
- edge_dst: int32 [8, 32768], P('rep', ('groups', 'dom')), parts along dimension 1, may hold values from 0 to 1023
- edge_src: int32 [8, 32768], P('rep', ('groups', 'dom')), parts along dimension 1, may hold values from 0 to 2047
- send_counts: int32 [8, 4], P(('groups', 'dom')), parts along dimension 0, may hold values from 1 to 512, as said below
- target_rows: int32 [32, 512], P(('groups', 'dom')), parts along dimension 0, may hold values from 0 to 2047
Outputs:
- grad_owned: float32 [16384, 512], P(('groups', 'dom'), 'rep'), parts along dimension 0
- grad_rel_weight: float32 [16, 512, 512], P(('groups', 'rep')), parts along dimension 0
There are 2 independent parts, one for each index of `groups`. A program takes and returns all parts, laid end to end along the dimension named above; an argument that names none is the same for every part. Nothing has to cross between parts.
Inputs may be any that keep to these rules, and one draw needn't show every extreme that they name: `send_counts`: each device has some owner to which all 512 of its slots are used.
All inputs are finite; a program needn't handle non-finite values.
Results may differ from a plain program's by a relative error of at most 0.0034.
Values sent between devices are 32-bit elements; how exact they have to be, the bound alone decides.
A program may use at most 128 MiB of HBM per device.

v0:
```python
import math

import jax
import jax.numpy as jnp
from jax import lax
from jax.sharding import PartitionSpec as P

OWN_DEV = 2048


def remap_slots(source, counts, slot_index, domain_count):
    block = source // slot_index
    position = source % slot_index
    picked = jnp.sum(
        jnp.where(block[:, None] == jnp.arange(domain_count)[None, :], counts[None, :], 0), axis=1
    )
    return block * slot_index + position % picked


def deliver(targets, arrived, owned_rows):
    step_rows = math.gcd(owned_rows, 512)
    starts = jnp.arange(0, owned_rows, step_rows, dtype=jnp.int32)

    def one_block(start):
        wanted = start + jnp.arange(step_rows, dtype=jnp.int32)
        picks = (targets[None, :] == wanted[:, None]).astype(jnp.float32)
        return jnp.dot(
            picks, arrived, precision=lax.Precision.HIGHEST, preferred_element_type=jnp.float32
        )

    blocks = lax.map(one_block, starts)
    return blocks.reshape(owned_rows, arrived.shape[1])


def on_device(
    grad_out, source_features, rel_weight, self_weight, edge_dst, edge_src, send_counts, target_rows
):
    domain_count = lax.axis_size("dom")
    slot_count = source_features.shape[0]
    slot_index = slot_count // domain_count
    destination_count = grad_out.shape[0]
    counts = send_counts[0]

    def one(pair):
        destination_relation, src_rel = pair
        fixed_portion = remap_slots(src_rel, counts, slot_index, domain_count)
        running_tally = (
            jnp.zeros((slot_count, destination_count), jnp.float32)
            .at[fixed_portion, destination_relation]
            .add(1.0)
        )
        degree = jnp.sum(running_tally, axis=0)
        norm = 1.0 / jnp.maximum(degree, 1.0)
        scaled = (grad_out.astype(jnp.float32) * norm[:, None]).astype(jnp.bfloat16)
        return jnp.dot(
            running_tally.astype(jnp.bfloat16), scaled, preferred_element_type=jnp.float32
        ).astype(jnp.bfloat16)

    pulled = lax.map(one, (edge_dst, edge_src))
    partial_value = jnp.einsum(
        "rso,rio->si", pulled, rel_weight, preferred_element_type=jnp.float32
    )
    weight_terms = jnp.einsum(
        "si,rso->rio", source_features, pulled, preferred_element_type=jnp.float32
    )
    grad_rel_weight = lax.psum(weight_terms, "dom")
    targets = target_rows.reshape(-1)
    arrived = lax.all_to_all(partial_value, "dom", split_axis=0, concat_axis=0, tiled=True)
    owned_full = deliver(targets, arrived, OWN_DEV)
    owned = lax.psum_scatter(owned_full, "rep", scatter_dimension=1, tiled=True)
    self_term = jnp.einsum("do,io->di", grad_out, self_weight, preferred_element_type=jnp.float32)
    owned = owned.at[:destination_count].add(self_term)
    return (owned, grad_rel_weight)


def solution(mesh):
    in_specs = (
        P(("groups", "dom"), None),
        P(("groups", "dom"), None),
        P("rep", None, None),
        P("rep", None),
        P("rep", ("groups", "dom")),
        P("rep", ("groups", "dom")),
        P(("groups", "dom"), None),
        P(("groups", "dom"), None),
    )
    out_specs = (P(("groups", "dom"), "rep"), P(("groups", "rep"), None, None))
    return jax.shard_map(
        on_device, mesh=mesh, in_specs=in_specs, out_specs=out_specs, check_vma=False
    )
```

profile of v0, /device:TPU:0, one launch (start us, length us, event | category | flops | bytes accessed | tf_op | source)
XLA Modules:
  0.0 355.7 jit_solution(6447269371448531562)
XLA Ops:
  8.0 103.1 %while.23 = (s32[]{:T(128)}, bf16[2,2048,512]{2,1,0:T(8,128)(2,1)}, s32[2,4096]{1,0:T(2,128)}, s32[1,4]{1,0:T(1,128)}, s32[2,4096]{1,0:T(2,128)}, /*index=5*/bf1...) while((s32[]{:T(128)}, bf16[2,2048,512]{2,1,0:T(8,128)(2,1)}, ...), condition=%wide.region_4.5_spmd, body=%wide.region_0.4_spmd.sunk | while | flops 2154624000 | bytes 49619644 | solution.py:59
  8.0 0.9 constant_dynamic-slice_fusion.2
  9.7 2.3 compare_select_fusion.7
  13.6 25.6 %scatter_custom_fusion.5 = f32[2097152]{0:T(1024)} fusion(s32[4096]{0:T(1024)S(1)} %broadcast_select_fusion.2, f32[4096]{0:T(1024)S(1)} %broadcast.363, f32[]{:T(128)} %constant.113.clone.1..sunk), kind=kCustom, calls=%fused_computation.8.clone.1 | custom fusion | flops 4096 | bytes 8388612 | tf_op jit(solution)/shard_map/while
  39.2 9.3 %reshape.280 = f32[2048,1024]{1,0:T(8,128)} reshape(f32[2097152]{0:T(1024)} %scatter_custom_fusion.5) | data formatting | bytes 16777216 | tf_op jit(solution)/shard_map/while/body/eval_jaxpr/scatter-add | solution.py:50
  48.5 4.0 %reduce_sum.30 = f32[1024]{0:T(1024)S(1)} reduce(f32[2048,1024]{1,0:T(8,128)} %reshape.280, f32[]{:T(128)} %constant.113.clone.1..sunk), dimensions={0}, to_apply=%region_3.3 | reduce | flops 2096128 | bytes 8392708 | tf_op jit(solution)/shard_map/while/body/eval_jaxpr/reduce_sum | solution.py:52
  52.5 7.2 %fusion.48 = bf16[2,2048,512]{2,1,0:T(8,128)(2,1)} fusion(bf16[2,2048,512]{2,1,0:T(8,128)(2,1)} %get-tuple-element.237, s32[]{:T(128)} %get-tuple-element.236, f32[2048,1024]{1,0:T(8,128)} %reshape.280, bf16[1024,512]{1,0:T(8,128)(2,1)S(1)} %copy-done.1, f32[1024]{0:T(1024)S(1)} %maximum_divide_fusion.2), kind=kOutput, calls=%fused_computation.14.clone.1 | convolution fusion | flops 2152202240 | bytes 11538944 | tf_op jit(solution)/shard_map/while/body/eval_jaxpr/dot_general | solution.py:55
  61.2 2.3 compare_select_fusion.7
  65.1 25.6 %scatter_custom_fusion.5 = f32[2097152]{0:T(1024)} fusion(s32[4096]{0:T(1024)S(1)} %broadcast_select_fusion.2, f32[4096]{0:T(1024)S(1)} %broadcast.363, f32[]{:T(128)} %constant.113.clone.1..sunk), kind=kCustom, calls=%fused_computation.8.clone.1 | custom fusion | flops 4096 | bytes 8388612 | tf_op jit(solution)/shard_map/while
  90.7 9.3 %reshape.280 = f32[2048,1024]{1,0:T(8,128)} reshape(f32[2097152]{0:T(1024)} %scatter_custom_fusion.5) | data formatting | bytes 16777216 | tf_op jit(solution)/shard_map/while/body/eval_jaxpr/scatter-add | solution.py:50
  100.0 4.0 %reduce_sum.30 = f32[1024]{0:T(1024)S(1)} reduce(f32[2048,1024]{1,0:T(8,128)} %reshape.280, f32[]{:T(128)} %constant.113.clone.1..sunk), dimensions={0}, to_apply=%region_3.3 | reduce | flops 2096128 | bytes 8392708 | tf_op jit(solution)/shard_map/while/body/eval_jaxpr/reduce_sum | solution.py:52
  104.0 7.1 %fusion.48 = bf16[2,2048,512]{2,1,0:T(8,128)(2,1)} fusion(bf16[2,2048,512]{2,1,0:T(8,128)(2,1)} %get-tuple-element.237, s32[]{:T(128)} %get-tuple-element.236, f32[2048,1024]{1,0:T(8,128)} %reshape.280, bf16[1024,512]{1,0:T(8,128)(2,1)S(1)} %copy-done.1, f32[1024]{0:T(1024)S(1)} %maximum_divide_fusion.2), kind=kOutput, calls=%fused_computation.14.clone.1 | convolution fusion | flops 2152202240 | bytes 11538944 | tf_op jit(solution)/shard_map/while/body/eval_jaxpr/dot_general | solution.py:55
  111.1 6.8 %fusion.33 = f32[2048,512,1]{1,0,2:T(8,128)} fusion(bf16[2,2048,512]{2,1,0:T(8,128)(2,1)} %get-tuple-element.121, bf16[2,512,512]{2,1,0:T(8,128)(2,1)} %param.16), kind=kOutput, calls=%fused_computation.49 | convolution fusion | flops 2147483648 | bytes 9437184 | tf_op jit(solution)/shard_map/rso,rio->si/dot_general | solution.py:60
  117.9 6.3 %all-to-all-start = ((f32[4,512,512]{2,1,0:T(8,128)}), f32[4,512,512]{2,1,0:T(8,128)}, u32[]{:S(2)}, u32[]{:S(2)}) async-start(f32[4,512,512]{2,1,0:T(8,128)} %bitcast.69), calls=%async_computation | async-start | bytes 8388608 | tf_op jit(solution)/shard_map/all_to_all | solution.py:68
  124.3 5.9 %fusion.29 = f32[2,512,512]{1,2,0:T(8,128)} fusion(bf16[2,2048,512]{2,1,0:T(8,128)(2,1)} %get-tuple-element.121, bf16[2048,512]{1,0:T(8,128)(2,1)S(1)} %copy-done), kind=kOutput, calls=%fused_computation.45 | convolution fusion | flops 2147483648 | bytes 8388608 | tf_op jit(solution)/shard_map/si,rso->rio/dot_general | solution.py:63
  130.4 137.8 %all-to-all-done = f32[4,512,512]{2,1,0:T(8,128)} async-done(((f32[4,512,512]{2,1,0:T(8,128)}), f32[4,512,512]{2,1,0:T(8,128)}, u32[]{:S(2)}, u32[]{:S(2)}) %all-to-all-start) | async-done | bytes 4194336 | tf_op jit(solution)/shard_map/all_to_all | solution.py:68
  268.2 32.6 %while.24 = (s32[]{:T(128)}, f32[4,512,512]{2,1,0:T(8,128)}, s32[4,512]{1,0:T(4,128)S(1)}, s32[4]{0:T(128)S(1)}, f32[2048,512]{1,0:T(8,128)}, /*index=5*/s32[]{:T(128)}) while((s32[]{:T(128)}, f32[4,512,512]{2,1,0:T(8,128)}, s32[4,512]{1,0:T(4,128)S(1)}, s32[4]{0:T(128)S(1)}, f32[2048,512]{1,0:T(8,128)}, /*index=5*/s32[]{:T(128)}) %tuple.63), condition=%wide.region_6.7_spmd, body=%wide.region_5.6_spmd.sunk | while | flops 6443500032 | bytes 5272149 | solution.py:31
  269.4 7.0 %fusion.51 = f32[4,512,512]{2,1,0:T(8,128)} fusion(f32[4,512,512]{2,1,0:T(8,128)} %get-tuple-element.265, s32[]{:T(128)} %get-tuple-element.264, f32[2048,512]{1,0:T(8,128)} %get-tuple-element.274, s32[2048]{0:T(1024)S(1)} %bitcast.74, s32[512]{0:T(512)S(1)} %iota_add_fusion.2), kind=kOutput, calls=%fused_computation.6.clone.1 | convolution fusion | flops 6443499520 | bytes 5253632 | tf_op jit(solution)/shard_map/while/body/eval_jaxpr/dot_general | solution.py:27
  277.7 6.9 %fusion.51 = f32[4,512,512]{2,1,0:T(8,128)} fusion(f32[4,512,512]{2,1,0:T(8,128)} %get-tuple-element.265, s32[]{:T(128)} %get-tuple-element.264, f32[2048,512]{1,0:T(8,128)} %get-tuple-element.274, s32[2048]{0:T(1024)S(1)} %bitcast.74, s32[512]{0:T(512)S(1)} %iota_add_fusion.2), kind=kOutput, calls=%fused_computation.6.clone.1 | convolution fusion | flops 6443499520 | bytes 5253632 | tf_op jit(solution)/shard_map/while/body/eval_jaxpr/dot_general | solution.py:27
  285.8 6.9 %fusion.51 = f32[4,512,512]{2,1,0:T(8,128)} fusion(f32[4,512,512]{2,1,0:T(8,128)} %get-tuple-element.265, s32[]{:T(128)} %get-tuple-element.264, f32[2048,512]{1,0:T(8,128)} %get-tuple-element.274, s32[2048]{0:T(1024)S(1)} %bitcast.74, s32[512]{0:T(512)S(1)} %iota_add_fusion.2), kind=kOutput, calls=%fused_computation.6.clone.1 | convolution fusion | flops 6443499520 | bytes 5253632 | tf_op jit(solution)/shard_map/while/body/eval_jaxpr/dot_general | solution.py:27
  293.9 6.9 %fusion.51 = f32[4,512,512]{2,1,0:T(8,128)} fusion(f32[4,512,512]{2,1,0:T(8,128)} %get-tuple-element.265, s32[]{:T(128)} %get-tuple-element.264, f32[2048,512]{1,0:T(8,128)} %get-tuple-element.274, s32[2048]{0:T(1024)S(1)} %bitcast.74, s32[512]{0:T(512)S(1)} %iota_add_fusion.2), kind=kOutput, calls=%fused_computation.6.clone.1 | convolution fusion | flops 6443499520 | bytes 5253632 | tf_op jit(solution)/shard_map/while/body/eval_jaxpr/dot_general | solution.py:27
  300.9 3.0 copy.15
  303.9 42.2 %reduce-scatter.2.cloned.1.call-done = f32[2048,128]{1,0:T(8,128)} async-done(((f32[2048,512]{1,0:T(8,128)}), f32[2048,128]{1,0:T(8,128)}) %reduce-scatter.2.cloned.1.call-update) | async-done | bytes 1048592 | tf_op jit(solution)/shard_map/reduce_scatter | solution.py:70
  346.0 2.3 fusion.32
  (47 shorter events, 10.6 us)
Async XLA Ops:
  8.0 116.3 %copy-start = (bf16[2048,512]{1,0:T(8,128)(2,1)S(1)}, bf16[2048,512]{1,0:T(8,128)(2,1)}, u32[]{:S(2)}) copy-start(bf16[2048,512]{1,0:T(8,128)(2,1)} %param.15) | copy-start | bytes 6291460
  48.5 4.0 %copy-start.1 = (bf16[1024,512]{1,0:T(8,128)(2,1)S(1)}, bf16[1024,512]{1,0:T(8,128)(2,1)}, u32[]{:S(2)}) copy-start(bf16[1024,512]{1,0:T(8,128)(2,1)} %get-tuple-element.252) | copy-start | bytes 3145732 | tf_op jit(solution)/shard_map/while
  100.0 4.0 %copy-start.1 = (bf16[1024,512]{1,0:T(8,128)(2,1)S(1)}, bf16[1024,512]{1,0:T(8,128)(2,1)}, u32[]{:S(2)}) copy-start(bf16[1024,512]{1,0:T(8,128)(2,1)} %get-tuple-element.252) | copy-start | bytes 3145732 | tf_op jit(solution)/shard_map/while
  117.9 150.3 %all-to-all-start = ((f32[4,512,512]{2,1,0:T(8,128)}), f32[4,512,512]{2,1,0:T(8,128)}, u32[]{:S(2)}, u32[]{:S(2)}) async-start(f32[4,512,512]{2,1,0:T(8,128)} %bitcast.69), calls=%async_computation | async-start | bytes 8388608 | tf_op jit(solution)/shard_map/all_to_all | solution.py:68
  124.2 144.0 %copy-start.3 = (s32[4,512]{1,0:T(4,128)S(1)}, s32[4,512]{1,0:T(4,128)}, u32[]{:S(2)}) copy-start(s32[4,512]{1,0:T(4,128)} %param.21) | copy-start | bytes 24580
  124.2 176.6 %all-reduce.2.cloned.1.call-start = ((), (), s32[]{:S(2)}) async-start(), calls=%async_computation.3 | async-start | bytes 4194304 | tf_op jit(solution)/shard_map/psum | solution.py:66
  130.1 215.9 %reduce-scatter.2.cloned.1.call-start = ((), (), s32[]{:S(2)}) async-start(), calls=%async_computation.2 | async-start | bytes 5242880 | tf_op jit(solution)/shard_map/reduce_scatter | solution.py:70
  300.8 45.2 %copy-start.2 = (bf16[1024,512]{1,0:T(8,128)(2,1)S(1)}, bf16[1024,512]{1,0:T(8,128)(2,1)}, u32[]{:S(2)}) copy-start(bf16[1024,512]{1,0:T(8,128)(2,1)} %get-tuple-element.285) | copy-start | bytes 3145732
  300.8 45.2 %copy-start.4 = (bf16[128,512]{1,0:T(8,128)(2,1)S(1)}, bf16[128,512]{1,0:T(8,128)(2,1)}, u32[]{:S(2)}) copy-start(bf16[128,512]{1,0:T(8,128)(2,1)} %param.17) | copy-start | bytes 393220
Sparse Core Ops, SparseCore 0:
  130.3 155.3 all-reduce.1
Sparse Core Ops, SparseCore 1:
  300.9 45.0 reduce-scatter.1
where the time goes:
time: 357 us; the launch traced here: 356 us
  waiting for transfers between devices  180 us (50%)
  other arithmetic  70.9 us (20%)
  matrix products  57 us (16%)
  local copies, waits for them, and re-layouts  25.6 us (7%)
  between operations  15.5 us (4%)
  starting transfers between devices  6.53 us (2%)
    all_to_all x1, waiting for transfers between devices, on_device(): lax.all_to_all(partial_value, 'dom', split_axis=0, concat_axis=0, tiled=T...  138 us
    while x8, other arithmetic  54.3 us
    reduce_scatter x1, waiting for transfers between devices, on_device(): owned = lax.psum_scatter(owned_full, 'rep', scatter_dimension=1, tiled=True)  42.2 us
    dot_general x4, matrix products, one_block(): jnp.dot(picks, arrived, precision=lax.Precision.HIGHEST, preferred_elemen...  27.7 us
    scatter-add x2, local copies, waits for them, and re-layouts, one(): running_tally = jnp.zeros((slot_count, destination_count), jnp.float32).a...  18.6 us
    dot_general x2, matrix products, one(): jnp.dot(running_tally.astype(jnp.bfloat16), scaled, preferred_element_typ...  14.3 us
    reduce_sum x2, other arithmetic, one(): degree = jnp.sum(running_tally, axis=0)  8 us
  transfers between devices with their start and end apart: 3, of which 2 were waited for; matrix products, arithmetic and copies ran while one was open for 12% of the time, Pallas kernels for 0%

commit v1 on v0

--- a/solution.py
+++ b/solution.py
@@ -60,14 +60,14 @@
     partial_value = jnp.einsum(
         "rso,rio->si", pulled, rel_weight, preferred_element_type=jnp.float32
     )
+    slot_grads = lax.psum_scatter(partial_value, "rep", scatter_dimension=1, tiled=True)
     weight_terms = jnp.einsum(
         "si,rso->rio", source_features, pulled, preferred_element_type=jnp.float32
     )
     grad_rel_weight = lax.psum(weight_terms, "dom")
     targets = target_rows.reshape(-1)
-    arrived = lax.all_to_all(partial_value, "dom", split_axis=0, concat_axis=0, tiled=True)
-    owned_full = deliver(targets, arrived, OWN_DEV)
-    owned = lax.psum_scatter(owned_full, "rep", scatter_dimension=1, tiled=True)
+    arrived = lax.all_to_all(slot_grads, "dom", split_axis=0, concat_axis=0, tiled=True)
+    owned = deliver(targets, arrived, OWN_DEV)
     self_term = jnp.einsum("do,io->di", grad_out, self_weight, preferred_element_type=jnp.float32)
     owned = owned.at[:destination_count].add(self_term)
     return (owned, grad_rel_weight)

time: 357 us -> 266 us (0.75)
  waiting for transfers between devices: 180 us -> 101 us
  matrix products: 57 us -> 43.8 us
    all_to_all x1, waiting for transfers between devices: 138 us -> 0.01 us  [on_device(): lax.all_to_all(slot_grads, 'dom', split_axis=0, concat_axis=0, tiled=True)]
    psum x1, waiting for transfers between devices: 0.02 us -> 59.9 us  [on_device(): grad_rel_weight = lax.psum(weight_terms, 'dom')]
    dot_general x4, matrix products: 27.7 us -> 15.6 us  [one_block(): jnp.dot(picks, arrived, precision=lax.Precision.HIGHEST, preferred_elemen...]
  transfers between devices with their start and end apart: 3 -> 3, of which waited for: 2 -> 2; matrix products, arithmetic and copies ran while one was open for 12% -> 3% of each run, Pallas kernels for 0% -> 0%
where the time goes in v1:
time: 266 us; the launch traced here: 265 us
  waiting for transfers between devices  101 us (38%)
  other arithmetic  71.2 us (27%)
  matrix products  43.8 us (16%)
  local copies, waits for them, and re-layouts  27.9 us (10%)
  between operations  15.5 us (6%)
  starting transfers between devices  4.7 us (2%)
    psum x1, waiting for transfers between devices, on_device(): grad_rel_weight = lax.psum(weight_terms, 'dom')  59.9 us
    while x8, other arithmetic  54.3 us
    reduce_scatter x1, waiting for transfers between devices, on_device(): lax.psum_scatter(partial_value, 'rep', scatter_dimension=1, tiled=True)  41.4 us
    scatter-add x2, local copies, waits for them, and re-layouts, one(): running_tally = jnp.zeros((slot_count, destination_count), jnp.float32).a...  18.6 us
    dot_general x4, matrix products, one_block(): jnp.dot(picks, arrived, precision=lax.Precision.HIGHEST, preferred_elemen...  15.6 us
    dot_general x2, matrix products, one(): jnp.dot(running_tally.astype(jnp.bfloat16), scaled, preferred_element_typ...  14.3 us
    reduce_sum x2, other arithmetic, one(): degree = jnp.sum(running_tally, axis=0)  8 us
    dot_general x1, matrix products, on_device(): jnp.einsum('rso,rio->si', pulled, rel_weight, preferred_element_type=jnp....  6.79 us
  transfers between devices with their start and end apart: 3, of which 2 were waited for; matrix products, arithmetic and copies ran while one was open for 3% of the time, Pallas kernels for 0%

profile of v1, /device:TPU:0, one launch (start us, length us, event | category | flops | bytes accessed | tf_op | source)
XLA Modules:
  0.0 264.7 jit_solution(3397538827962022508)
XLA Ops:
  8.1 103.1 %while.23 = (s32[]{:T(128)}, bf16[2,2048,512]{2,1,0:T(8,128)(2,1)}, s32[2,4096]{1,0:T(2,128)}, s32[1,4]{1,0:T(1,128)}, s32[2,4096]{1,0:T(2,128)}, /*index=5*/bf1...) while((s32[]{:T(128)}, bf16[2,2048,512]{2,1,0:T(8,128)(2,1)}, ...), condition=%wide.region_4.5_spmd, body=%wide.region_0.4_spmd.sunk | while | flops 2154624000 | bytes 49619644 | solution.py:59
  9.8 2.3 compare_select_fusion.7
  13.6 25.6 %scatter_custom_fusion.5 = f32[2097152]{0:T(1024)} fusion(s32[4096]{0:T(1024)S(1)} %broadcast_select_fusion.2, f32[4096]{0:T(1024)S(1)} %broadcast.363, f32[]{:T(128)} %constant.113.clone.1..sunk), kind=kCustom, calls=%fused_computation.8.clone.1 | custom fusion | flops 4096 | bytes 8388612 | tf_op jit(solution)/shard_map/while
  39.2 9.3 %reshape.284 = f32[2048,1024]{1,0:T(8,128)} reshape(f32[2097152]{0:T(1024)} %scatter_custom_fusion.5) | data formatting | bytes 16777216 | tf_op jit(solution)/shard_map/while/body/eval_jaxpr/scatter-add | solution.py:50
  48.5 4.0 %reduce_sum.30 = f32[1024]{0:T(1024)S(1)} reduce(f32[2048,1024]{1,0:T(8,128)} %reshape.284, f32[]{:T(128)} %constant.113.clone.1..sunk), dimensions={0}, to_apply=%region_3.3 | reduce | flops 2096128 | bytes 8392708 | tf_op jit(solution)/shard_map/while/body/eval_jaxpr/reduce_sum | solution.py:52
  52.5 7.2 %fusion.47 = bf16[2,2048,512]{2,1,0:T(8,128)(2,1)} fusion(bf16[2,2048,512]{2,1,0:T(8,128)(2,1)} %get-tuple-element.237, s32[]{:T(128)} %get-tuple-element.236, f32[2048,1024]{1,0:T(8,128)} %reshape.284, bf16[1024,512]{1,0:T(8,128)(2,1)S(1)} %copy-done.1, f32[1024]{0:T(1024)S(1)} %maximum_divide_fusion.2), kind=kOutput, calls=%fused_computation.14.clone.1 | convolution fusion | flops 2152202240 | bytes 11538944 | tf_op jit(solution)/shard_map/while/body/eval_jaxpr/dot_general | solution.py:55
  61.3 2.3 compare_select_fusion.7
  65.1 25.6 %scatter_custom_fusion.5 = f32[2097152]{0:T(1024)} fusion(s32[4096]{0:T(1024)S(1)} %broadcast_select_fusion.2, f32[4096]{0:T(1024)S(1)} %broadcast.363, f32[]{:T(128)} %constant.113.clone.1..sunk), kind=kCustom, calls=%fused_computation.8.clone.1 | custom fusion | flops 4096 | bytes 8388612 | tf_op jit(solution)/shard_map/while
  90.7 9.3 %reshape.284 = f32[2048,1024]{1,0:T(8,128)} reshape(f32[2097152]{0:T(1024)} %scatter_custom_fusion.5) | data formatting | bytes 16777216 | tf_op jit(solution)/shard_map/while/body/eval_jaxpr/scatter-add | solution.py:50
  100.0 4.0 %reduce_sum.30 = f32[1024]{0:T(1024)S(1)} reduce(f32[2048,1024]{1,0:T(8,128)} %reshape.284, f32[]{:T(128)} %constant.113.clone.1..sunk), dimensions={0}, to_apply=%region_3.3 | reduce | flops 2096128 | bytes 8392708 | tf_op jit(solution)/shard_map/while/body/eval_jaxpr/reduce_sum | solution.py:52
  104.0 7.1 %fusion.47 = bf16[2,2048,512]{2,1,0:T(8,128)(2,1)} fusion(bf16[2,2048,512]{2,1,0:T(8,128)(2,1)} %get-tuple-element.237, s32[]{:T(128)} %get-tuple-element.236, f32[2048,1024]{1,0:T(8,128)} %reshape.284, bf16[1024,512]{1,0:T(8,128)(2,1)S(1)} %copy-done.1, f32[1024]{0:T(1024)S(1)} %maximum_divide_fusion.2), kind=kOutput, calls=%fused_computation.14.clone.1 | convolution fusion | flops 2152202240 | bytes 11538944 | tf_op jit(solution)/shard_map/while/body/eval_jaxpr/dot_general | solution.py:55
  111.1 6.8 %convolution_bitcast_fusion = f32[2048,512]{1,0:T(8,128)} fusion(bf16[2,2048,512]{2,1,0:T(8,128)(2,1)} %get-tuple-element.121, bf16[2,512,512]{2,1,0:T(8,128)(2,1)} %param.16), kind=kOutput, calls=%fused_computation.43 | convolution fusion | flops 2147483648 | bytes 9437184 | tf_op jit(solution)/shard_map/rso,rio->si/dot_general | solution.py:60
  118.0 5.9 %fusion.29 = f32[2,512,512]{1,2,0:T(8,128)} fusion(bf16[2,2048,512]{2,1,0:T(8,128)(2,1)} %get-tuple-element.121, bf16[2048,512]{1,0:T(8,128)(2,1)S(1)} %copy-done), kind=kOutput, calls=%fused_computation.46 | convolution fusion | flops 2147483648 | bytes 8388608 | tf_op jit(solution)/shard_map/si,rso->rio/dot_general | solution.py:64
  123.9 41.4 %reduce-scatter.2.cloned.1.call-done = f32[2048,128]{1,0:T(8,128)} async-done(((f32[2048,512]{1,0:T(8,128)}), f32[2048,128]{1,0:T(8,128)}) %reduce-scatter.2.cloned.1.call-update) | async-done | bytes 1048592 | tf_op jit(solution)/shard_map/reduce_scatter | solution.py:63
  165.3 4.6 %all-to-all-start = ((f32[4,512,128]{2,1,0:T(8,128)}), f32[4,512,128]{2,1,0:T(8,128)S(1)}, u32[]{:S(2)}, u32[]{:S(2)}) async-start(f32[4,512,128]{2,1,0:T(8,128)} %bitcast.74), calls=%async_computation.1 | async-start | bytes 2097152 | tf_op jit(solution)/shard_map/all_to_all | solution.py:69
  170.0 59.9 %all-reduce.2.cloned.1.call-done = f32[2,512,512]{1,2,0:T(8,128)} async-done(((f32[2,512,512]{1,2,0:T(8,128)}), f32[2,512,512]{1,2,0:T(8,128)}) %all-reduce.2.cloned.1.call-update) | async-done | bytes 2097168 | tf_op jit(solution)/shard_map/psum | solution.py:67
  229.9 2.9 %copy.15 = f32[2,512,512]{2,1,0:T(8,128)} copy(f32[2,512,512]{1,2,0:T(8,128)} %all-reduce.2.cloned.1.call-done) | data formatting | bytes 4194304
  233.7 21.1 %while.24 = (s32[]{:T(128)}, f32[4,512,128]{2,1,0:T(8,128)}, s32[4,512]{1,0:T(4,128)S(1)}, s32[4]{0:T(128)S(1)}, f32[2048,128]{1,0:T(8,128)}, /*index=5*/s32[]{:T(128)}) while((s32[]{:T(128)}, f32[4,512,128]{2,1,0:T(8,128)}, s32[4,512]{1,0:T(4,128)S(1)}, s32[4]{0:T(128)S(1)}, f32[2048,128]{1,0:T(8,128)}, /*index=5*/s32[]{:T(128)}) %tuple.64), condition=%wide.region_7.8_spmd, body=%wide.region_6.7_spmd.sunk | while | flops 1611661824 | bytes 1339989 | solution.py:31
  235.1 3.9 %fusion.50 = f32[4,512,128]{2,1,0:T(8,128)} fusion(f32[4,512,128]{2,1,0:T(8,128)} %get-tuple-element.265, s32[]{:T(128)} %get-tuple-element.264, f32[2048,128]{1,0:T(8,128)} %get-tuple-element.274, s32[2048]{0:T(1024)S(1)} %bitcast.77, s32[512]{0:T(512)S(1)} %iota_add_fusion.2), kind=kOutput, calls=%fused_computation.6.clone.1 | convolution fusion | flops 1611661312 | bytes 1321472 | tf_op jit(solution)/shard_map/while/body/eval_jaxpr/dot_general | solution.py:27
  240.4 3.9 %fusion.50 = f32[4,512,128]{2,1,0:T(8,128)} fusion(f32[4,512,128]{2,1,0:T(8,128)} %get-tuple-element.265, s32[]{:T(128)} %get-tuple-element.264, f32[2048,128]{1,0:T(8,128)} %get-tuple-element.274, s32[2048]{0:T(1024)S(1)} %bitcast.77, s32[512]{0:T(512)S(1)} %iota_add_fusion.2), kind=kOutput, calls=%fused_computation.6.clone.1 | convolution fusion | flops 1611661312 | bytes 1321472 | tf_op jit(solution)/shard_map/while/body/eval_jaxpr/dot_general | solution.py:27
  245.7 3.9 %fusion.50 = f32[4,512,128]{2,1,0:T(8,128)} fusion(f32[4,512,128]{2,1,0:T(8,128)} %get-tuple-element.265, s32[]{:T(128)} %get-tuple-element.264, f32[2048,128]{1,0:T(8,128)} %get-tuple-element.274, s32[2048]{0:T(1024)S(1)} %bitcast.77, s32[512]{0:T(512)S(1)} %iota_add_fusion.2), kind=kOutput, calls=%fused_computation.6.clone.1 | convolution fusion | flops 1611661312 | bytes 1321472 | tf_op jit(solution)/shard_map/while/body/eval_jaxpr/dot_general | solution.py:27
  251.0 3.9 %fusion.50 = f32[4,512,128]{2,1,0:T(8,128)} fusion(f32[4,512,128]{2,1,0:T(8,128)} %get-tuple-element.265, s32[]{:T(128)} %get-tuple-element.264, f32[2048,128]{1,0:T(8,128)} %get-tuple-element.274, s32[2048]{0:T(1024)S(1)} %bitcast.77, s32[512]{0:T(512)S(1)} %iota_add_fusion.2), kind=kOutput, calls=%fused_computation.6.clone.1 | convolution fusion | flops 1611661312 | bytes 1321472 | tf_op jit(solution)/shard_map/while/body/eval_jaxpr/dot_general | solution.py:27
  254.9 1.1 slice.20
  256.0 1.2 fusion.32
  (50 shorter events, 13.0 us)
Async XLA Ops:
  8.0 110.0 %copy-start = (bf16[2048,512]{1,0:T(8,128)(2,1)S(1)}, bf16[2048,512]{1,0:T(8,128)(2,1)}, u32[]{:S(2)}) copy-start(bf16[2048,512]{1,0:T(8,128)(2,1)} %param.15) | copy-start | bytes 6291460
  8.0 157.3 %reduce-scatter.2.cloned.1.call-start = ((), (), s32[]{:S(2)}) async-start(), calls=%async_computation.2 | async-start | bytes 5242880 | tf_op jit(solution)/shard_map/reduce_scatter | solution.py:63
  48.5 4.0 %copy-start.1 = (bf16[1024,512]{1,0:T(8,128)(2,1)S(1)}, bf16[1024,512]{1,0:T(8,128)(2,1)}, u32[]{:S(2)}) copy-start(bf16[1024,512]{1,0:T(8,128)(2,1)} %get-tuple-element.252) | copy-start | bytes 3145732 | tf_op jit(solution)/shard_map/while
  100.0 4.0 %copy-start.1 = (bf16[1024,512]{1,0:T(8,128)(2,1)S(1)}, bf16[1024,512]{1,0:T(8,128)(2,1)}, u32[]{:S(2)}) copy-start(bf16[1024,512]{1,0:T(8,128)(2,1)} %get-tuple-element.252) | copy-start | bytes 3145732 | tf_op jit(solution)/shard_map/while
  118.0 111.9 %all-reduce.2.cloned.1.call-start = ((), (), s32[]{:S(2)}) async-start(), calls=%async_computation.3 | async-start | bytes 4194304 | tf_op jit(solution)/shard_map/psum | solution.py:67
  123.9 109.9 %copy-start.4 = (s32[4,512]{1,0:T(4,128)S(1)}, s32[4,512]{1,0:T(4,128)}, u32[]{:S(2)}) copy-start(s32[4,512]{1,0:T(4,128)} %param.21) | copy-start | bytes 24580
  165.3 67.4 %all-to-all-start = ((f32[4,512,128]{2,1,0:T(8,128)}), f32[4,512,128]{2,1,0:T(8,128)S(1)}, u32[]{:S(2)}, u32[]{:S(2)}) async-start(f32[4,512,128]{2,1,0:T(8,128)} %bitcast.74), calls=%async_computation.1 | async-start | bytes 2097152 | tf_op jit(solution)/shard_map/all_to_all | solution.py:69
  232.7 1.0 copy-start.3
  233.7 22.2 %copy-start.2 = (bf16[1024,512]{1,0:T(8,128)(2,1)S(1)}, bf16[1024,512]{1,0:T(8,128)(2,1)}, u32[]{:S(2)}) copy-start(bf16[1024,512]{1,0:T(8,128)(2,1)} %get-tuple-element.283) | copy-start | bytes 3145732
  233.7 22.2 %copy-start.5 = (bf16[128,512]{1,0:T(8,128)(2,1)S(1)}, bf16[128,512]{1,0:T(8,128)(2,1)}, u32[]{:S(2)}) copy-start(bf16[128,512]{1,0:T(8,128)(2,1)} %param.17) | copy-start | bytes 393220
Sparse Core Ops, SparseCore 0:
  118.1 47.2 reduce-scatter.1
Sparse Core Ops, SparseCore 1:
  124.0 105.8 all-reduce.1

commit v2 on v1

v2 whole, which is shorter than its diff:
```python
import math

import jax
import jax.numpy as jnp
from jax import lax
from jax.experimental import pallas as pl
from jax.experimental.pallas import tpu as pltpu
from jax.sharding import PartitionSpec as P

OWN_DEV = 2048
TN = (((0,), (0,)), ((), ()))
NT = (((1,), (1,)), ((), ()))


def remap_slots(source, counts, slot_index, domain_count):
    block = source // slot_index
    position = source % slot_index
    picked = jnp.sum(
        jnp.where(block[..., None] == jnp.arange(domain_count), counts, 0), axis=-1
    )
    return block * slot_index + position % picked


def pick(first, rows, wanted):
    places = first + lax.broadcasted_iota(jnp.int32, (rows, wanted.shape[1]), 0)
    return jnp.where(places == wanted, 1.0, 0.0).astype(jnp.bfloat16)


def pull_kernel(dst_ref, slot_ref, grad_ref, pulled_ref, scaled, rows):
    destinations, width = grad_ref.shape
    edges = dst_ref.shape[1]
    tile = pulled_ref.shape[0]
    step = pl.program_id(0)

    @pl.when(step == 0)
    def _():
        block = math.gcd(destinations, 128)

        @pl.loop(0, destinations // block)
        def _(i):
            first = pl.multiple_of(i * block, block)
            places = first + lax.broadcasted_iota(jnp.int32, (block, edges), 0)
            hits = jnp.where(places == dst_ref[...], 1.0, 0.0)
            degree = jnp.sum(hits, axis=1, keepdims=True)
            norm = 1.0 / jnp.maximum(degree, 1.0)
            here = pl.ds(first, block)
            values = grad_ref[here, :].astype(jnp.float32) * norm
            scaled[:, here] = values.T.astype(jnp.bfloat16)

        chunk = math.gcd(edges, 512)

        @pl.loop(0, edges // chunk)
        def _(i):
            here = pl.ds(pl.multiple_of(i * chunk, chunk), chunk)
            picks = pick(0, destinations, dst_ref[:, here])
            rows[:, here] = jnp.dot(
                scaled[...], picks, preferred_element_type=jnp.float32
            ).astype(jnp.bfloat16)

    picks = pick(step * tile, tile, slot_ref[...])
    pulled_ref[...] = lax.dot_general(
        picks, rows[...], NT, preferred_element_type=jnp.float32
    ).astype(jnp.bfloat16)


def pull(dst, slots, grad_out, slot_count):
    destinations, width = grad_out.shape
    edges = dst.shape[1]
    tile = math.gcd(slot_count, 256)
    return pl.pallas_call(
        pull_kernel,
        grid=(slot_count // tile,),
        out_shape=jax.ShapeDtypeStruct((slot_count, width), jnp.bfloat16),
        in_specs=[
            pl.BlockSpec((1, edges), lambda i: (0, 0)),
            pl.BlockSpec((1, edges), lambda i: (0, 0)),
            pl.BlockSpec((destinations, width), lambda i: (0, 0)),
        ],
        out_specs=pl.BlockSpec((tile, width), lambda i: (i, 0)),
        scratch_shapes=[
            pltpu.VMEM((width, destinations), jnp.bfloat16),
            pltpu.VMEM((width, edges), jnp.bfloat16),
        ],
        compiler_params=pltpu.CompilerParams(vmem_limit_bytes=40 * 2**20),
        cost_estimate=pl.CostEstimate(
            flops=2 * edges * width * (destinations + slot_count),
            bytes_accessed=2 * width * (destinations + slot_count),
            transcendentals=0,
        ),
    )(dst, slots, grad_out)


def deliver_kernel(self_steps, targets_ref, arrived_ref, self_ref, owned_ref, parts):
    tile, width = owned_ref.shape
    step = pl.program_id(0)

    @pl.when(step == 0)
    def _():
        rest = arrived_ref[...]
        for i in range(3):
            part = rest.astype(jnp.bfloat16)
            parts[:, i * width : (i + 1) * width] = part
            rest = rest - part.astype(jnp.float32)

    picks = pick(step * tile, tile, targets_ref[...])
    sums = jnp.dot(picks, parts[...], preferred_element_type=jnp.float32)
    total = sums[:, 2 * width :] + sums[:, width : 2 * width] + sums[:, :width]
    owned_ref[...] = total + jnp.where(step < self_steps, self_ref[...], 0.0)


def deliver(targets, arrived, self_term, owned_rows):
    count, width = arrived.shape
    tile = math.gcd(self_term.shape[0], math.gcd(owned_rows, 512))
    self_steps = self_term.shape[0] // tile
    return pl.pallas_call(
        lambda *refs: deliver_kernel(self_steps, *refs),
        grid=(owned_rows // tile,),
        out_shape=jax.ShapeDtypeStruct((owned_rows, width), jnp.float32),
        in_specs=[
            pl.BlockSpec((1, count), lambda i: (0, 0)),
            pl.BlockSpec((count, width), lambda i: (0, 0)),
            pl.BlockSpec((tile, width), lambda i: (jnp.minimum(i, self_steps - 1), 0)),
        ],
        out_specs=pl.BlockSpec((tile, width), lambda i: (i, 0)),
        scratch_shapes=[pltpu.VMEM((count, 3 * width), jnp.bfloat16)],
        compiler_params=pltpu.CompilerParams(vmem_limit_bytes=32 * 2**20),
        cost_estimate=pl.CostEstimate(
            flops=6 * count * width * owned_rows,
            bytes_accessed=4 * width * (count + owned_rows),
            transcendentals=0,
        ),
    )(targets, arrived, self_term)


def on_device(
    grad_out, source_features, rel_weight, self_weight, edge_dst, edge_src, send_counts, target_rows
):
    domain_count = lax.axis_size("dom")
    slot_count = source_features.shape[0]
    slot_index = slot_count // domain_count
    slots = remap_slots(edge_src, send_counts[0], slot_index, domain_count)
    relations = rel_weight.shape[0]

    pulled, weight_grads = [], []
    for r in range(relations):
        here = pull(edge_dst[r : r + 1], slots[r : r + 1], grad_out, slot_count)
        terms = lax.dot_general(source_features, here, TN, preferred_element_type=jnp.float32)
        pulled.append(here)
        weight_grads.append(lax.psum(terms, "dom"))
    partial_value = sum(
        lax.dot_general(pulled[r], rel_weight[r], NT, preferred_element_type=jnp.float32)
        for r in range(relations)
    )
    slot_grads = lax.psum_scatter(partial_value, "rep", scatter_dimension=1, tiled=True)
    arrived = lax.all_to_all(slot_grads, "dom", split_axis=0, concat_axis=0, tiled=True)
    self_term = lax.dot_general(grad_out, self_weight, NT, preferred_element_type=jnp.float32)
    owned = deliver(target_rows.reshape(1, -1), arrived, self_term, OWN_DEV)
    return (owned, jnp.stack(weight_grads))


def solution(mesh):
    in_specs = (
        P(("groups", "dom"), None),
        P(("groups", "dom"), None),
        P("rep", None, None),
        P("rep", None),
        P("rep", ("groups", "dom")),
        P("rep", ("groups", "dom")),
        P(("groups", "dom"), None),
        P(("groups", "dom"), None),
    )
    out_specs = (P(("groups", "dom"), "rep"), P(("groups", "rep"), None, None))
    return jax.shard_map(
        on_device, mesh=mesh, in_specs=in_specs, out_specs=out_specs, check_vma=False
    )
```

time: 266 us -> 192 us (0.72)
  other arithmetic: 71.2 us -> 7.04 us
  Pallas kernels: 0 us -> 44.3 us
  matrix products: 43.8 us -> 13.2 us
  local copies, waits for them, and re-layouts: 27.9 us -> 7.41 us
    while x8 -> x0, other arithmetic: 54.3 us -> none
    pallas_call x0 -> x3, Pallas kernels: none -> 44.3 us  [the longest x2 38.2 us: pull(): pl.pallas_call(pull_kernel, grid=(slot_count // tile,), out_shape=jax.Sha...]
    dot_general x9 -> x5, matrix products: 43.8 us -> 13.2 us  [the longest x2 6.22 us: on_device(): lax.dot_general(source_features, here, TN, preferred_element_type=jnp.flo...]
    scatter-add x2 -> x0, local copies, waits for them, and re-layouts: 18.6 us -> none  [one(): running_tally = jnp.zeros((slot_count, destination_count), jnp.float32).a...]
    reduce_sum x4 -> x1, other arithmetic: 9.53 us -> 0.83 us  [remap_slots(): jnp.sum(jnp.where(block[..., None] == jnp.arange(domain_count), counts, 0...]
    select_n x2 -> x0, other arithmetic: 4.53 us -> none  [one(): running_tally = jnp.zeros((slot_count, destination_count), jnp.float32).a...]
    dynamic_slice x6 -> x0, local copies, waits for them, and re-layouts: 4.32 us -> none  [the longest x4 2.64 us: deliver(): blocks = lax.map(one_block, starts)]
    another operation x0 -> x1, other arithmetic: none -> 3.04 us  [on_device(): return (owned, jnp.stack(weight_grads))]
  transfers between devices with their start and end apart: 3 -> 3, of which waited for: 2 -> 2; matrix products, arithmetic and copies ran while one was open for 3% -> 8% of each run, Pallas kernels for 0% -> 0%
where the time goes in v2:
time: 192 us; the launch traced here: 191 us
  waiting for transfers between devices  98.8 us (51%)
  Pallas kernels  44.3 us (23%)
  between operations  15.6 us (8%)
  matrix products  13.2 us (7%)
  local copies, waits for them, and re-layouts  7.41 us (4%)
  other arithmetic  7.04 us (4%)
  starting transfers between devices  4.68 us (2%)
    psum x1, waiting for transfers between devices, on_device(): weight_grads.append(lax.psum(terms, 'dom'))  57.7 us
    reduce_scatter x1, waiting for transfers between devices, on_device(): lax.psum_scatter(partial_value, 'rep', scatter_dimension=1, tiled=True)  41.1 us
    pallas_call x2, Pallas kernels, pull(): pl.pallas_call(pull_kernel, grid=(slot_count // tile,), out_shape=jax.Sha...  38.2 us
    unnamed x20, local copies, waits for them, and re-layouts  6.52 us
    dot_general x2, matrix products, on_device(): lax.dot_general(source_features, here, TN, preferred_element_type=jnp.flo...  6.22 us
    pallas_call x1, Pallas kernels, deliver(): pl.pallas_call(lambda *refs: deliver_kernel(self_steps, *refs), grid=(own...  6.09 us
    all_to_all x1, starting transfers between devices, on_device(): lax.all_to_all(slot_grads, 'dom', split_axis=0, concat_axis=0, tiled=True)  4.6 us
    dot_general x2, matrix products, on_device(): lax.dot_general(pulled[r], rel_weight[r], NT, preferred_element_type=jnp....  4.52 us
  transfers between devices with their start and end apart: 3, of which 2 were waited for; matrix products, arithmetic and copies ran while one was open for 8% of the time, Pallas kernels for 0%

profile of v2, /device:TPU:0, one launch (start us, length us, event | category | flops | bytes accessed | tf_op | source)
XLA Modules:
  0.0 191.0 jit_solution(10639814872732657099)
XLA Ops:
  8.0 0.0 reduce-scatter.2.cloned.1.call-start
  8.1 1.0 and_select_fusion.2
  9.0 0.8 select_reduce_fusion
  9.9 2.2 %multiply_add_fusion = s32[2,4096]{1,0:T(2,128)S(1)} fusion(s32[2,4096]{1,0:T(2,128)S(1)} %select_reduce_fusion, s32[2,4096]{1,0:T(2,128)} %param.13), kind=kLoop, calls=%fused_computation.18 | loop fusion | flops 253952 | bytes 98304 | tf_op jit(solution)/shard_map/add | solution.py:21
  12.1 0.9 fusion.5
  13.0 1.2 copy-done.4
  14.2 19.1 %shard_map.95 = bf16[2048,512]{1,0:T(8,128)(2,1)S(1)} custom-call(s32[1,4096]{1,0:T(1,128)S(1)} %get-tuple-element.12.dst_ref, s32[1,4096]{1,0:T(1,128)S(1)} %get-tuple-element.9.slot_ref, bf16[1024,512]{1,0:T(8,128)(2,1)S(1)} %copy-done.4), custom_call_target="tpu_custom_call" | custom-call | flops 12884901888 | bytes 3145728 | tf_op jit(solution)/shard_map/pallas_call | solution.py:70
  33.3 1.3 fusion.1
  34.6 0.0 copy-done.2
  34.6 19.1 %shard_map.96 = bf16[2048,512]{1,0:T(8,128)(2,1)S(1)} custom-call(s32[1,4096]{1,0:T(1,128)S(1)} %get-tuple-element.13.dst_ref, s32[1,4096]{1,0:T(1,128)S(1)} %get-tuple-element.8.slot_ref, bf16[1024,512]{1,0:T(8,128)(2,1)S(1)} %copy-done.4), custom_call_target="tpu_custom_call" | custom-call | flops 12884901888 | bytes 3145728 | tf_op jit(solution)/shard_map/pallas_call | solution.py:70
  53.8 1.3 copy-done.1
  55.1 3.2 %convolution_add_fusion = f32[2048,512]{1,0:T(8,128)} fusion(f32[2048,512]{1,0:T(8,128)S(1)} %fusion.1, bf16[2048,512]{1,0:T(8,128)(2,1)S(1)} %shard_map.96, bf16[2,512,512]{2,1,0:T(8,128)(2,1)S(1)} %copy-done.6), kind=kOutput, calls=%fused_computation | convolution fusion | flops 1074790400 | bytes 11010048 | tf_op jit(solution)/shard_map/dot_general | solution.py:151
  58.3 0.0 all-reduce.3.cloned.1.call-start
  58.4 4.0 %convolution_bitcast_fusion = f32[1,512,512]{1,2,0:T(8,128)} fusion(bf16[2048,512]{1,0:T(8,128)(2,1)} %copy-done.1, bf16[2048,512]{1,0:T(8,128)(2,1)S(1)} %copy-done), kind=kOutput, calls=%fused_computation.2 | convolution fusion | flops 1073741824 | bytes 5242880 | tf_op jit(solution)/shard_map/dot_general | solution.py:147
  62.4 2.2 %convolution_bitcast_fusion.1 = f32[1,512,512]{1,2,0:T(8,128)} fusion(bf16[2048,512]{1,0:T(8,128)(2,1)S(1)} %copy-done.3, bf16[2048,512]{1,0:T(8,128)(2,1)S(1)} %copy-done), kind=kOutput, calls=%fused_computation.3 | convolution fusion | flops 1073741824 | bytes 5242880 | tf_op jit(solution)/shard_map/dot_general | solution.py:147
  64.6 0.0 all-reduce.3.cloned.1.call-update
  64.7 41.1 %reduce-scatter.2.cloned.1.call-done = f32[2048,128]{1,0:T(8,128)} async-done(((f32[2048,512]{1,0:T(8,128)}), f32[2048,128]{1,0:T(8,128)}) %reduce-scatter.2.cloned.1.call-update) | async-done | bytes 1048592 | tf_op jit(solution)/shard_map/reduce_scatter | solution.py:154
  105.7 4.6 %all-to-all-start = ((f32[4,512,128]{2,1,0:T(8,128)}), f32[4,512,128]{2,1,0:T(8,128)S(1)}, u32[]{:S(2)}, u32[]{:S(2)}) async-start(f32[4,512,128]{2,1,0:T(8,128)} %bitcast.30), calls=%async_computation.1 | async-start | bytes 2097152 | tf_op jit(solution)/shard_map/all_to_all | solution.py:155
  110.4 2.5 %fusion.7.refs_2_ = f32[1024,128]{1,0:T(8,128)} fusion(bf16[1024,512]{1,0:T(8,128)(2,1)} %grad_ref.3, bf16[128,512]{1,0:T(8,128)(2,1)S(1)} %copy-done.7), kind=kOutput, calls=%fused_computation.23 | convolution fusion | flops 134217728 | bytes 1703936 | tf_op jit(solution)/shard_map/dot_general | solution.py:156
  112.8 57.7 %all-reduce.3.cloned.1.call-done = (f32[1,512,512]{1,2,0:T(8,128)}, f32[1,512,512]{1,2,0:T(8,128)}) async-done(((f32[1,512,512]{1,2,0:T(8,128)}, f32[1,512,512]{1,2,0:T(8,128)}), (f32[1,512,512]{1,2,0:T(8,128)}, f32[1,512,512]{1,2,0:T(8,128)})) %all-reduce.3.cloned.1.call-update) | async-done | bytes 2097168 | tf_op jit(solution)/shard_map/psum | solution.py:149
  170.5 3.0 %pad_maximum_fusion = f32[2,512,512]{1,2,0:T(8,128)} fusion(f32[1,512,512]{1,2,0:T(8,128)} %get-tuple-element.6, f32[1,512,512]{1,2,0:T(8,128)} %get-tuple-element.7), kind=kLoop, calls=%fused_computation.1 | loop fusion | flops 524288 | bytes 4194304 | tf_op jit(solution)/shard_map/stack | solution.py:158
  173.5 2.9 %copy.11 = f32[2,512,512]{2,1,0:T(8,128)} copy(f32[2,512,512]{1,2,0:T(8,128)} %pad_maximum_fusion) | data formatting | bytes 4194304
  176.4 1.0 copy-done.5
  177.5 6.1 %shard_map.97 = f32[2048,128]{1,0:T(8,128)} custom-call(s32[1,2048]{1,0:T(1,128)S(1)} %bitcast.29, f32[2048,128]{1,0:T(8,128)S(1)} %bitcast.28, f32[1024,128]{1,0:T(8,128)S(1)} %copy-done.5), custom_call_target="tpu_custom_call" | custom-call | flops 3221225472 | bytes 2097152 | tf_op jit(solution)/shard_map/pallas_call | solution.py:115
  (17 shorter events, 0.1 us)
Async XLA Ops:
  8.0 50.4 %copy-start = (bf16[2048,512]{1,0:T(8,128)(2,1)S(1)}, bf16[2048,512]{1,0:T(8,128)(2,1)}, u32[]{:S(2)}) copy-start(bf16[2048,512]{1,0:T(8,128)(2,1)} %param.9) | copy-start | bytes 6291460
  8.0 97.7 %reduce-scatter.2.cloned.1.call-start = ((), (), s32[]{:S(2)}) async-start(), calls=%async_computation.2 | async-start | bytes 5242880 | tf_op jit(solution)/shard_map/reduce_scatter | solution.py:154
  13.0 1.2 copy-start.4
  14.2 19.1 %copy-start.6 = (bf16[2,512,512]{2,1,0:T(8,128)(2,1)S(1)}, bf16[2,512,512]{2,1,0:T(8,128)(2,1)}, u32[]{:S(2)}) copy-start(bf16[2,512,512]{2,1,0:T(8,128)(2,1)} %param.10) | copy-start | bytes 3145732
  33.3 1.3 copy-start.2
  53.7 1.3 copy-start.1
  58.3 112.2 %all-reduce.3.cloned.1.call-start = ((), (), s32[]{:S(2)}) async-start(), calls=%async_computation.3 | async-start | bytes 4194304 | tf_op jit(solution)/shard_map/psum | solution.py:149
  58.4 4.0 %copy-start.3 = (bf16[2048,512]{1,0:T(8,128)(2,1)S(1)}, bf16[2048,512]{1,0:T(8,128)(2,1)}, u32[]{:S(2)}) copy-start(bf16[2048,512]{1,0:T(8,128)(2,1)} %copy-done.2) | copy-start | bytes 6291460
  64.6 45.7 %copy-start.8 = (s32[4,512]{1,0:T(4,128)S(1)}, s32[4,512]{1,0:T(4,128)}, u32[]{:S(2)}) copy-start(s32[4,512]{1,0:T(4,128)} %param.15) | copy-start | bytes 24580
  64.6 45.7 %copy-start.7 = (bf16[128,512]{1,0:T(8,128)(2,1)S(1)}, bf16[128,512]{1,0:T(8,128)(2,1)}, u32[]{:S(2)}) copy-start(bf16[128,512]{1,0:T(8,128)(2,1)} %param.11) | copy-start | bytes 393220
  105.7 70.7 %all-to-all-start = ((f32[4,512,128]{2,1,0:T(8,128)}), f32[4,512,128]{2,1,0:T(8,128)S(1)}, u32[]{:S(2)}, u32[]{:S(2)}) async-start(f32[4,512,128]{2,1,0:T(8,128)} %bitcast.30), calls=%async_computation.1 | async-start | bytes 2097152 | tf_op jit(solution)/shard_map/all_to_all | solution.py:155
  176.4 1.0 copy-start.5
Sparse Core Ops, SparseCore 0:
  58.5 47.2 reduce-scatter.1
Sparse Core Ops, SparseCore 1:
  64.7 105.7 all-reduce.2

commit v3 on v2

--- a/solution.py
+++ b/solution.py
@@ -26,7 +26,9 @@
     return jnp.where(places == wanted, 1.0, 0.0).astype(jnp.bfloat16)
 
 
-def pull_kernel(dst_ref, slot_ref, grad_ref, pulled_ref, scaled, rows):
+def pull_kernel(
+    dst_ref, slot_ref, grad_ref, feature_ref, pulled_ref, weight_ref, scaled, rows
+):
     destinations, width = grad_ref.shape
     edges = dst_ref.shape[1]
     tile = pulled_ref.shape[0]
@@ -34,6 +36,7 @@
 
     @pl.when(step == 0)
     def _():
+        weight_ref[...] = jnp.zeros_like(weight_ref)
         block = math.gcd(destinations, 128)
 
         @pl.loop(0, destinations // block)
@@ -58,25 +61,37 @@
             ).astype(jnp.bfloat16)
 
     picks = pick(step * tile, tile, slot_ref[...])
-    pulled_ref[...] = lax.dot_general(
+    pulled = lax.dot_general(
         picks, rows[...], NT, preferred_element_type=jnp.float32
     ).astype(jnp.bfloat16)
-
-
-def pull(dst, slots, grad_out, slot_count):
+    pulled_ref[...] = pulled
+    weight_ref[...] += lax.dot_general(
+        feature_ref[...], pulled, TN, preferred_element_type=jnp.float32
+    )
+
+
+def pull(dst, slots, grad_out, features):
     destinations, width = grad_out.shape
+    slot_count, inputs = features.shape
     edges = dst.shape[1]
     tile = math.gcd(slot_count, 256)
     return pl.pallas_call(
         pull_kernel,
         grid=(slot_count // tile,),
-        out_shape=jax.ShapeDtypeStruct((slot_count, width), jnp.bfloat16),
+        out_shape=(
+            jax.ShapeDtypeStruct((slot_count, width), jnp.bfloat16),
+            jax.ShapeDtypeStruct((inputs, width), jnp.float32),
+        ),
         in_specs=[
             pl.BlockSpec((1, edges), lambda i: (0, 0)),
             pl.BlockSpec((1, edges), lambda i: (0, 0)),
             pl.BlockSpec((destinations, width), lambda i: (0, 0)),
+            pl.BlockSpec((tile, inputs), lambda i: (i, 0)),
         ],
-        out_specs=pl.BlockSpec((tile, width), lambda i: (i, 0)),
+        out_specs=(
+            pl.BlockSpec((tile, width), lambda i: (i, 0)),
+            pl.BlockSpec((inputs, width), lambda i: (0, 0)),
+        ),
         scratch_shapes=[
             pltpu.VMEM((width, destinations), jnp.bfloat16),
             pltpu.VMEM((width, edges), jnp.bfloat16),
@@ -84,10 +99,61 @@
         compiler_params=pltpu.CompilerParams(vmem_limit_bytes=40 * 2**20),
         cost_estimate=pl.CostEstimate(
             flops=2 * edges * width * (destinations + slot_count),
-            bytes_accessed=2 * width * (destinations + slot_count),
+            bytes_accessed=2 * width * (destinations + 2 * slot_count + 2 * inputs),
             transcendentals=0,
         ),
-    )(dst, slots, grad_out)
+    )(dst, slots, grad_out, features)
+
+
+def sum_over_line(value, axis):
+    count = lax.axis_size(axis)
+    if count % 2 or count > 8:
+        return lax.psum(value, axis)
+    me = lax.axis_index(axis)
+    middle = count // 2
+    for hop in range(middle - 1):
+        pairs = [(hop, hop + 1), (count - 1 - hop, count - 2 - hop)]
+        value = value + lax.ppermute(value, axis, pairs)
+    value = value + lax.ppermute(value, axis, [(middle - 1, middle), (middle, middle - 1)])
+    for hop in range(middle - 1):
+        low, high = middle - 2 - hop, middle + 1 + hop
+        given = lax.ppermute(value, axis, [(low + 1, low), (high - 1, high)])
+        value = jnp.where((me == low) | (me == high), given, value)
+    return value
+
+
+def project(pulled, weights):
+    return sum(
+        lax.dot_general(p, w, NT, preferred_element_type=jnp.float32)
+        for p, w in zip(pulled, weights)
+    )
+
+
+def project_and_scatter(pulled, rel_weight, axis):
+    if lax.axis_size(axis) != 4:
+        return lax.psum_scatter(
+            project(pulled, rel_weight), axis, scatter_dimension=1, tiled=True
+        )
+    me = lax.axis_index(axis)
+    high, low = me // 2, me % 2
+    relations, inputs, outputs = rel_weight.shape
+    quarters = rel_weight.reshape(relations, 2, 2, inputs // 4, outputs)
+
+    def half(at_low):
+        one = lambda at_high: lax.dynamic_slice(
+            quarters,
+            (0, at_high, at_low, 0, 0),
+            (relations, 1, 1, inputs // 4, outputs),
+        ).reshape(relations, inputs // 4, outputs)
+        return jnp.concatenate([one(1 - high), one(high)], axis=1)
+
+    sent = project(pulled, half(1 - low))
+    given = lax.ppermute(sent, axis, [(i, i ^ 1) for i in range(4)])
+    kept = project(pulled, half(low))
+    width = inputs // 4
+    crossing = kept[:, :width] + given[:, :width]
+    crossed = lax.ppermute(crossing, axis, [(i, i ^ 2) for i in range(4)])
+    return kept[:, width:] + given[:, width:] + crossed
 
 
 def deliver_kernel(self_steps, targets_ref, arrived_ref, self_ref, owned_ref, parts):
@@ -136,22 +202,17 @@
     grad_out, source_features, rel_weight, self_weight, edge_dst, edge_src, send_counts, target_rows
 ):
     domain_count = lax.axis_size("dom")
-    slot_count = source_features.shape[0]
-    slot_index = slot_count // domain_count
+    slot_index = source_features.shape[0] // domain_count
     slots = remap_slots(edge_src, send_counts[0], slot_index, domain_count)
     relations = rel_weight.shape[0]
 
     pulled, weight_grads = [], []
     for r in range(relations):
-        here = pull(edge_dst[r : r + 1], slots[r : r + 1], grad_out, slot_count)
-        terms = lax.dot_general(source_features, here, TN, preferred_element_type=jnp.float32)
+        here, terms = pull(edge_dst[r : r + 1], slots[r : r + 1], grad_out, source_features)
         pulled.append(here)
-        weight_grads.append(lax.psum(terms, "dom"))
-    partial_value = sum(
-        lax.dot_general(pulled[r], rel_weight[r], NT, preferred_element_type=jnp.float32)
-        for r in range(relations)
-    )
-    slot_grads = lax.psum_scatter(partial_value, "rep", scatter_dimension=1, tiled=True)
+        pieces = [sum_over_line(piece, "dom") for piece in jnp.split(terms, 2, axis=0)]
+        weight_grads.append(jnp.concatenate(pieces, axis=0))
+    slot_grads = project_and_scatter(pulled, rel_weight, "rep")
     arrived = lax.all_to_all(slot_grads, "dom", split_axis=0, concat_axis=0, tiled=True)
     self_term = lax.dot_general(grad_out, self_weight, NT, preferred_element_type=jnp.float32)
     owned = deliver(target_rows.reshape(1, -1), arrived, self_term, OWN_DEV)

time: 192 us -> 188 us (0.979)
  starting transfers between devices: 4.68 us -> 29.9 us
  waiting for transfers between devices: 98.8 us -> 82.1 us
  between operations: 15.6 us -> 0.99 us
  matrix products: 13.2 us -> 3.38 us
  other arithmetic: 7.04 us -> 14.1 us
  Pallas kernels: 44.3 us -> 48.9 us
    ppermute x0 -> x14, waiting for transfers between devices: none -> 82.1 us  [the longest x4 45.9 us: sum_over_line(): given = lax.ppermute(value, axis, [(low + 1, low), (high - 1, high)])]
    psum x1 -> x0, waiting for transfers between devices: 57.7 us -> none  [on_device(): weight_grads.append(lax.psum(terms, 'dom'))]
    reduce_scatter x1 -> x0, waiting for transfers between devices: 41.1 us -> none  [on_device(): lax.psum_scatter(partial_value, 'rep', scatter_dimension=1, tiled=True)]
    ppermute x0 -> x14, starting transfers between devices: none -> 20.4 us  [the longest x4 8.88 us: sum_over_line(): value = value + lax.ppermute(value, axis, pairs)]
    dot_general x4, matrix products: 10.7 us -> 2.96 us  [project(): lax.dot_general(p, w, NT, preferred_element_type=jnp.float32)]
    add x0 -> x8, other arithmetic: none -> 6.21 us  [the longest x4 3.53 us: sum_over_line(): value + lax.ppermute(value, axis, [(middle - 1, middle), (middle, middle...]
    all_to_all x1, starting transfers between devices: 4.6 us -> 9.43 us  [on_device(): lax.all_to_all(slot_grads, 'dom', split_axis=0, concat_axis=0, tiled=True)]
    pallas_call x2, Pallas kernels: 38.2 us -> 42.8 us  [pull(): pl.pallas_call(pull_kernel, grid=(slot_count // tile,), out_shape=(jax.Sh...]
  transfers between devices with their start and end apart: 3 -> 15, of which waited for: 2 -> 8; matrix products, arithmetic and copies ran while one was open for 8% -> 7% of each run, Pallas kernels for 0% -> 0%
where the time goes in v3:
time: 188 us
  waiting for transfers between devices  82.1 us (44%)
  Pallas kernels  48.9 us (26%)
  starting transfers between devices  29.9 us (16%)
  other arithmetic  14.1 us (8%)
  local copies, waits for them, and re-layouts  8.25 us (4%)
  matrix products  3.38 us (2%)
    ppermute x4, waiting for transfers between devices, sum_over_line(): given = lax.ppermute(value, axis, [(low + 1, low), (high - 1, high)])  45.9 us
    pallas_call x2, Pallas kernels, pull(): pl.pallas_call(pull_kernel, grid=(slot_count // tile,), out_shape=(jax.Sh...  42.8 us
    ppermute x4, waiting for transfers between devices, sum_over_line(): value = value + lax.ppermute(value, axis, pairs)  36.2 us
    all_to_all x1, starting transfers between devices, on_device(): lax.all_to_all(slot_grads, 'dom', split_axis=0, concat_axis=0, tiled=True)  9.43 us
    ppermute x4, starting transfers between devices, sum_over_line(): value = value + lax.ppermute(value, axis, pairs)  8.88 us
    pallas_call x1, Pallas kernels, deliver(): pl.pallas_call(lambda *refs: deliver_kernel(self_steps, *refs), grid=(own...  6.09 us
    unnamed x21, local copies, waits for them, and re-layouts  5.96 us
    ppermute x4, starting transfers between devices, sum_over_line(): given = lax.ppermute(value, axis, [(low + 1, low), (high - 1, high)])  5.16 us
  transfers between devices with their start and end apart: 15, of which 8 were waited for; matrix products, arithmetic and copies ran while one was open for 7% of the time, Pallas kernels for 0%

profile of v3, /device:TPU:0, one launch (start us, length us, event | category | flops | bytes accessed | tf_op | source)
XLA Modules:
  0.0 187.6 jit_solution(16847793897191639386)
XLA Ops:
  2.4 2.2 %multiply_add_fusion = s32[2,4096]{1,0:T(2,128)S(1)} fusion(s32[2,4096]{1,0:T(2,128)S(1)} %select_reduce_fusion, s32[2,4096]{1,0:T(2,128)} %param.13), kind=kLoop, calls=%fused_computation.41 | loop fusion | flops 253952 | bytes 98304 | tf_op jit(solution)/shard_map/add | solution.py:21
  6.7 1.6 copy-done.8
  8.3 21.4 %shard_map.95 = (bf16[2048,512]{1,0:T(8,128)(2,1)S(1)}, f32[512,512]{1,0:T(8,128)S(1)}) custom-call(s32[1,4096]{1,0:T(1,128)S(1)} %get-tuple-element.26.dst_ref, s32[1,4096]{1,0:T(1,128)S(1)} %get-tuple-element.23.slot_ref, bf16[1024,512]{1,0:T(8,128)(2,1)S(1)} %copy-done.5, bf16[2048,512]{1,0:T(8,128)(2,1)S(1)} %copy-done.8), custom_call_target="tpu_custom_call" | custom-call | flops 12884901888 | bytes 6291456 | tf_op jit(solution)/shard_map/pallas_call | solution.py:78
  30.7 21.4 %shard_map.96 = (bf16[2048,512]{1,0:T(8,128)(2,1)S(1)}, f32[512,512]{1,0:T(8,128)S(1)}) custom-call(s32[1,4096]{1,0:T(1,128)S(1)} %get-tuple-element.27.dst_ref, s32[1,4096]{1,0:T(1,128)S(1)} %get-tuple-element.22.slot_ref, bf16[1024,512]{1,0:T(8,128)(2,1)S(1)} %copy-done.6, bf16[2048,512]{1,0:T(8,128)(2,1)S(1)} %copy-done.8), custom_call_target="tpu_custom_call" | custom-call | flops 12884901888 | bytes 6291456 | tf_op jit(solution)/shard_map/pallas_call | solution.py:78
  52.1 1.3 copy-done.1
  57.6 4.9 %collective-permute-start.2 = (f32[256,512]{1,0:T(8,128)S(1)}, f32[256,512]{1,0:T(8,128)S(1)}, u32[]{:S(2)}, u32[]{:S(2)}) collective-permute-start(f32[256,512]{1,0:T(8,128)S(1)} %get-tuple-element.12), channel_id=1, source_target_pairs={{0,4},{12,8},{1,5},{13,9},{2,6},{14,10},{3,7},{15,11},{16,20},{28,... | collective-permute-start | bytes 1572872 | tf_op jit(solution)/shard_map/ppermute | solution.py:116
  62.5 1.3 collective-permute-start.5
  65.5 1.6 collective-permute-start.1
  67.1 1.3 collective-permute-start.11
  68.4 1.3 collective-permute-start.8
  69.8 5.0 %collective-permute-done.2 = f32[256,512]{1,0:T(8,128)S(1)} collective-permute-done((f32[256,512]{1,0:T(8,128)S(1)}, f32[256,512]{1,0:T(8,128)S(1)}, u32[]{:S(2)}, u32[]{:S(2)}) %collective-permute-start.2) | collective-permute-done | bytes 524320 | tf_op jit(solution)/shard_map/ppermute | solution.py:116
  74.8 11.2 %collective-permute-done.5 = f32[256,512]{1,0:T(8,128)S(1)} collective-permute-done((f32[256,512]{1,0:T(8,128)S(1)}, f32[256,512]{1,0:T(8,128)S(1)}, u32[]{:S(2)}, u32[]{:S(2)}) %collective-permute-start.5) | collective-permute-done | bytes 524320 | tf_op jit(solution)/shard_map/ppermute | solution.py:116
  87.6 9.6 %collective-permute-done.11 = f32[256,512]{1,0:T(8,128)S(1)} collective-permute-done((f32[256,512]{1,0:T(8,128)S(1)}, f32[256,512]{1,0:T(8,128)S(1)}, u32[]{:S(2)}, u32[]{:S(2)}) %collective-permute-start.11) | collective-permute-done | bytes 524320 | tf_op jit(solution)/shard_map/ppermute | solution.py:116
  97.2 10.4 %collective-permute-done.8 = f32[256,512]{1,0:T(8,128)S(1)} collective-permute-done((f32[256,512]{1,0:T(8,128)S(1)}, f32[256,512]{1,0:T(8,128)S(1)}, u32[]{:S(2)}, u32[]{:S(2)}) %collective-permute-start.8) | collective-permute-done | bytes 524320 | tf_op jit(solution)/shard_map/ppermute | solution.py:116
  108.8 1.4 collective-permute-start.9
  110.3 1.5 collective-permute-start.12
  111.8 1.3 collective-permute-start.4
  116.5 9.4 %all-to-all-start = ((f32[4,512,128]{2,1,0:T(8,128)}), f32[4,512,128]{2,1,0:T(8,128)S(1)}, u32[]{:S(2)}, u32[]{:S(2)}) async-start(f32[4,512,128]{2,1,0:T(8,128)} %bitcast.10), calls=%async_computation | async-start | bytes 2097152 | tf_op jit(solution)/shard_map/all_to_all | solution.py:216
  131.6 5.3 %collective-permute-done.4 = f32[256,512]{1,0:T(8,128)} collective-permute-done((f32[256,512]{1,0:T(8,128)S(1)}, f32[256,512]{1,0:T(8,128)}, u32[]{:S(2)}, u32[]{:S(2)}) %collective-permute-start.4) | collective-permute-done | bytes 524320 | tf_op jit(solution)/shard_map/ppermute | solution.py:120
  138.0 10.3 %collective-permute-done.7 = f32[256,512]{1,0:T(8,128)} collective-permute-done((f32[256,512]{1,0:T(8,128)}, f32[256,512]{1,0:T(8,128)}, u32[]{:S(2)}, u32[]{:S(2)}) %collective-permute-start.7) | collective-permute-done | bytes 524320 | tf_op jit(solution)/shard_map/ppermute | solution.py:120
  149.5 21.2 %collective-permute-done.10 = f32[256,512]{1,0:T(8,128)S(1)} collective-permute-done((f32[256,512]{1,0:T(8,128)S(1)}, f32[256,512]{1,0:T(8,128)S(1)}, u32[]{:S(2)}, u32[]{:S(2)}) %collective-permute-start.10) | collective-permute-done | bytes 524320 | tf_op jit(solution)/shard_map/ppermute | solution.py:120
  170.8 9.1 %collective-permute-done.13 = f32[256,512]{1,0:T(8,128)S(1)} collective-permute-done((f32[256,512]{1,0:T(8,128)S(1)}, f32[256,512]{1,0:T(8,128)S(1)}, u32[]{:S(2)}, u32[]{:S(2)}) %collective-permute-start.13) | collective-permute-done | bytes 524320 | tf_op jit(solution)/shard_map/ppermute | solution.py:120
  180.0 1.5 pad_maximum_fusion
  181.5 6.1 %shard_map.97 = f32[2048,128]{1,0:T(8,128)} custom-call(s32[1,2048]{1,0:T(1,128)S(1)} %bitcast.38, f32[2048,128]{1,0:T(8,128)S(1)} %bitcast.37, f32[1024,128]{1,0:T(8,128)S(1)} %fusion.23.refs_2_), custom_call_target="tpu_custom_call" | custom-call | flops 3221225472 | bytes 2097152 | tf_op jit(solution)/shard_map/pallas_call | solution.py:181
  (57 shorter events, 25.0 us)
Async XLA Ops:
  0.6 125.3 %copy-start = (bf16[128,512]{1,0:T(8,128)(2,1)S(1)}, bf16[128,512]{1,0:T(8,128)(2,1)}, u32[]{:S(2)}) copy-start(bf16[128,512]{1,0:T(8,128)(2,1)} %param.11) | copy-start | bytes 393220
  5.5 1.2 copy-start.5
  6.7 1.6 copy-start.8
  8.3 22.4 %copy-start.6 = (bf16[1024,512]{1,0:T(8,128)(2,1)S(1)}, bf16[1024,512]{1,0:T(8,128)(2,1)}, u32[]{:S(2)}) copy-start(bf16[1024,512]{1,0:T(8,128)(2,1)} %grad_ref.3) | copy-start | bytes 3145732
  52.1 1.3 copy-start.1
  54.7 1.6 copy-start.2
  56.2 1.3 copy-start.4
  57.0 8.3 %collective-permute-start = (f32[2048,256]{1,0:T(8,128)S(1)}, f32[2048,256]{1,0:T(8,128)S(1)}, u32[]{:S(2)}, u32[]{:S(2)}) collective-permute-start(f32[2048,256]{1,0:T(8,128)S(1)} %convolution_add_fusion), channel_id=1, source_target_pairs={{0,1},{1,0},{2,3},{3,2},{4,5},{5,4},{6,7},{7,6},{8,9},{9,8},{10,11... | collective-permute-start | bytes 6291464 | tf_op jit(solution)/shard_map/ppermute | solution.py:151
  57.6 17.2 %collective-permute-start.2 = (f32[256,512]{1,0:T(8,128)S(1)}, f32[256,512]{1,0:T(8,128)S(1)}, u32[]{:S(2)}, u32[]{:S(2)}) collective-permute-start(f32[256,512]{1,0:T(8,128)S(1)} %get-tuple-element.12), channel_id=1, source_target_pairs={{0,4},{12,8},{1,5},{13,9},{2,6},{14,10},{3,7},{15,11},{16,20},{28,... | collective-permute-start | bytes 1572872 | tf_op jit(solution)/shard_map/ppermute | solution.py:116
  62.5 23.5 %collective-permute-start.5 = (f32[256,512]{1,0:T(8,128)S(1)}, f32[256,512]{1,0:T(8,128)S(1)}, u32[]{:S(2)}, u32[]{:S(2)}) collective-permute-start(f32[256,512]{1,0:T(8,128)S(1)} %get-tuple-element.13), channel_id=1, source_target_pairs={{0,4},{12,8},{1,5},{13,9},{2,6},{14,10},{3,7},{15,11},{16,20},{28,... | collective-permute-start | bytes 1572872 | tf_op jit(solution)/shard_map/ppermute | solution.py:116
  65.5 49.8 %collective-permute-start.1 = (f32[2048,128]{1,0:T(8,128)S(1)}, f32[2048,128]{1,0:T(8,128)S(1)}, u32[]{:S(2)}, u32[]{:S(2)}) collective-permute-start(f32[2048,128]{1,0:T(8,128)S(1)} %slice_add_fusion), channel_id=1, source_target_pairs={{0,2},{1,3},{2,0},{3,1},{4,6},{5,7},{6,4},{7,5},{8,10},{9,11},{10,... | collective-permute-start | bytes 3145736 | tf_op jit(solution)/shard_map/ppermute | solution.py:155
  67.1 30.1 %collective-permute-start.11 = (f32[256,512]{1,0:T(8,128)S(1)}, f32[256,512]{1,0:T(8,128)S(1)}, u32[]{:S(2)}, u32[]{:S(2)}) collective-permute-start(f32[256,512]{1,0:T(8,128)S(1)} %get-tuple-element.17), channel_id=1, source_target_pairs={{0,4},{12,8},{1,5},{13,9},{2,6},{14,10},{3,7},{15,11},{16,20},{28,... | collective-permute-start | bytes 1572872 | tf_op jit(solution)/shard_map/ppermute | solution.py:116
  68.4 39.2 %collective-permute-start.8 = (f32[256,512]{1,0:T(8,128)S(1)}, f32[256,512]{1,0:T(8,128)S(1)}, u32[]{:S(2)}, u32[]{:S(2)}) collective-permute-start(f32[256,512]{1,0:T(8,128)S(1)} %get-tuple-element.16), channel_id=1, source_target_pairs={{0,4},{12,8},{1,5},{13,9},{2,6},{14,10},{3,7},{15,11},{16,20},{28,... | collective-permute-start | bytes 1572872 | tf_op jit(solution)/shard_map/ppermute | solution.py:116
  86.2 25.5 %collective-permute-start.3 = (f32[256,512]{1,0:T(8,128)S(1)}, f32[256,512]{1,0:T(8,128)S(1)}, u32[]{:S(2)}, u32[]{:S(2)}) collective-permute-start(f32[256,512]{1,0:T(8,128)S(1)} %get-tuple-element.10), channel_id=1, source_target_pairs={{4,8},{8,4},{5,9},{9,5},{6,10},{10,6},{7,11},{11,7},{20,24},{24,20... | collective-permute-start | bytes 1572872 | tf_op jit(solution)/shard_map/ppermute | solution.py:117
  86.9 26.2 %collective-permute-start.6 = (f32[256,512]{1,0:T(8,128)S(1)}, f32[256,512]{1,0:T(8,128)S(1)}, u32[]{:S(2)}, u32[]{:S(2)}) collective-permute-start(f32[256,512]{1,0:T(8,128)S(1)} %get-tuple-element.11), channel_id=1, source_target_pairs={{4,8},{8,4},{5,9},{9,5},{6,10},{10,6},{7,11},{11,7},{20,24},{24,20... | collective-permute-start | bytes 1572872 | tf_op jit(solution)/shard_map/ppermute | solution.py:117
  108.8 17.6 %collective-permute-start.9 = (f32[256,512]{1,0:T(8,128)}, f32[256,512]{1,0:T(8,128)}, u32[]{:S(2)}, u32[]{:S(2)}) collective-permute-start(f32[256,512]{1,0:T(8,128)} %get-tuple-element.14), channel_id=1, source_target_pairs={{4,8},{8,4},{5,9},{9,5},{6,10},{10,6},{7,11},{11,7},{20,24},{24,20... | collective-permute-start | bytes 1572872 | tf_op jit(solution)/shard_map/ppermute | solution.py:117
  110.3 18.7 %collective-permute-start.12 = (f32[256,512]{1,0:T(8,128)}, f32[256,512]{1,0:T(8,128)}, u32[]{:S(2)}, u32[]{:S(2)}) collective-permute-start(f32[256,512]{1,0:T(8,128)} %get-tuple-element.15), channel_id=1, source_target_pairs={{4,8},{8,4},{5,9},{9,5},{6,10},{10,6},{7,11},{11,7},{20,24},{24,20... | collective-permute-start | bytes 1572872 | tf_op jit(solution)/shard_map/ppermute | solution.py:117
  111.8 25.1 %collective-permute-start.4 = (f32[256,512]{1,0:T(8,128)S(1)}, f32[256,512]{1,0:T(8,128)}, u32[]{:S(2)}, u32[]{:S(2)}) collective-permute-start(f32[256,512]{1,0:T(8,128)S(1)} %add.90), channel_id=1, source_target_pairs={{4,0},{8,12},{5,1},{9,13},{6,2},{10,14},{7,3},{11,15},{20,16},{24,... | collective-permute-start | bytes 1572872 | tf_op jit(solution)/shard_map/ppermute | solution.py:120
  114.0 34.3 %collective-permute-start.7 = (f32[256,512]{1,0:T(8,128)}, f32[256,512]{1,0:T(8,128)}, u32[]{:S(2)}, u32[]{:S(2)}) collective-permute-start(f32[256,512]{1,0:T(8,128)} %add.92), channel_id=1, source_target_pairs={{4,0},{8,12},{5,1},{9,13},{6,2},{10,14},{7,3},{11,15},{20,16},{24,... | collective-permute-start | bytes 1572872 | tf_op jit(solution)/shard_map/ppermute | solution.py:120
  116.5 9.4 %copy-start.7 = (bf16[1024,512]{1,0:T(8,128)(2,1)S(1)}, bf16[1024,512]{1,0:T(8,128)(2,1)}, u32[]{:S(2)}) copy-start(bf16[1024,512]{1,0:T(8,128)(2,1)} %grad_ref.3) | copy-start | bytes 3145732
  116.5 9.9 %copy-start.9 = (s32[4,512]{1,0:T(4,128)S(1)}, s32[4,512]{1,0:T(4,128)}, u32[]{:S(2)}) copy-start(s32[4,512]{1,0:T(4,128)} %param.15) | copy-start | bytes 24580
  116.5 65.1 %all-to-all-start = ((f32[4,512,128]{2,1,0:T(8,128)}), f32[4,512,128]{2,1,0:T(8,128)S(1)}, u32[]{:S(2)}, u32[]{:S(2)}) async-start(f32[4,512,128]{2,1,0:T(8,128)} %bitcast.10), calls=%async_computation | async-start | bytes 2097152 | tf_op jit(solution)/shard_map/all_to_all | solution.py:216
  127.7 43.0 %collective-permute-start.10 = (f32[256,512]{1,0:T(8,128)S(1)}, f32[256,512]{1,0:T(8,128)S(1)}, u32[]{:S(2)}, u32[]{:S(2)}) collective-permute-start(f32[256,512]{1,0:T(8,128)S(1)} %add.94), channel_id=1, source_target_pairs={{4,0},{8,12},{5,1},{9,13},{6,2},{10,14},{7,3},{11,15},{20,16},{24,... | collective-permute-start | bytes 1572872 | tf_op jit(solution)/shard_map/ppermute | solution.py:120
  130.3 49.6 %collective-permute-start.13 = (f32[256,512]{1,0:T(8,128)S(1)}, f32[256,512]{1,0:T(8,128)S(1)}, u32[]{:S(2)}, u32[]{:S(2)}) collective-permute-start(f32[256,512]{1,0:T(8,128)S(1)} %add.96), channel_id=1, source_target_pairs={{4,0},{8,12},{5,1},{9,13},{6,2},{10,14},{7,3},{11,15},{20,16},{24,... | collective-permute-start | bytes 1572872 | tf_op jit(solution)/shard_map/ppermute | solution.py:120
  (1 other events, 1.0 us)

commit v4 on v3

--- a/solution.py
+++ b/solution.py
@@ -105,21 +105,39 @@
     )(dst, slots, grad_out, features)
 
 
-def sum_over_line(value, axis):
+def sum_over_line(groups, axis):
     count = lax.axis_size(axis)
     if count % 2 or count > 8:
-        return lax.psum(value, axis)
+        return [lax.psum(piece, axis) for group in groups for piece in group]
     me = lax.axis_index(axis)
     middle = count // 2
-    for hop in range(middle - 1):
-        pairs = [(hop, hop + 1), (count - 1 - hop, count - 2 - hop)]
-        value = value + lax.ppermute(value, axis, pairs)
-    value = value + lax.ppermute(value, axis, [(middle - 1, middle), (middle, middle - 1)])
-    for hop in range(middle - 1):
-        low, high = middle - 2 - hop, middle + 1 + hop
-        given = lax.ppermute(value, axis, [(low + 1, low), (high - 1, high)])
-        value = jnp.where((me == low) | (me == high), given, value)
-    return value
+    right = [(i, i + 1) for i in range(count - 1)]
+    left = [(i + 1, i) for i in range(count - 1)]
+    pieces = sum(len(group) for group in groups)
+    held = groups[0]
+    later = list(groups[1:])
+
+    def choose(number):
+        value = held[0]
+        for k in range(1, len(held)):
+            value = jnp.where(number >= k, held[k], value)
+        return value
+
+    for step in range(pieces + count - 2):
+        if step == len(held) and later:
+            held = held + later.pop(0)
+        from_left = lax.ppermute(choose(step - me), axis, right)
+        from_right = lax.ppermute(choose(step - (count - 1 - me)), axis, left)
+        at_left, at_right = step - me + 1, step - (count - 1 - me) + 1
+        new = []
+        for k, value in enumerate(held):
+            by_left = jnp.where(me <= middle, value + from_left, from_left)
+            value = jnp.where((at_left == k) & (me > 0), by_left, value)
+            by_right = jnp.where(me >= middle - 1, value + from_right, from_right)
+            value = jnp.where((at_right == k) & (me < count - 1), by_right, value)
+            new.append(value)
+        held = new
+    return held
 
 
 def project(pulled, weights):
@@ -206,17 +224,18 @@
     slots = remap_slots(edge_src, send_counts[0], slot_index, domain_count)
     relations = rel_weight.shape[0]
 
-    pulled, weight_grads = [], []
+    pulled, groups = [], []
     for r in range(relations):
         here, terms = pull(edge_dst[r : r + 1], slots[r : r + 1], grad_out, source_features)
         pulled.append(here)
-        pieces = [sum_over_line(piece, "dom") for piece in jnp.split(terms, 2, axis=0)]
-        weight_grads.append(jnp.concatenate(pieces, axis=0))
+        groups.append(list(jnp.split(terms, 2, axis=0)))
+    pieces = sum_over_line(groups, "dom")
+    weight_grads = jnp.concatenate(pieces, axis=0).reshape(rel_weight.shape)
     slot_grads = project_and_scatter(pulled, rel_weight, "rep")
     arrived = lax.all_to_all(slot_grads, "dom", split_axis=0, concat_axis=0, tiled=True)
     self_term = lax.dot_general(grad_out, self_weight, NT, preferred_element_type=jnp.float32)
     owned = deliver(target_rows.reshape(1, -1), arrived, self_term, OWN_DEV)
-    return (owned, jnp.stack(weight_grads))
+    return (owned, weight_grads)
 
 
 def solution(mesh):

time: 188 us -> 187 us (level)
  the two profiles are of different devices: /device:TPU:0 before, /device:TPU:14 now
where the time goes in v4:
time: 187 us; the launch traced here: 186 us
  Pallas kernels  48.9 us (26%)
  waiting for transfers between devices  45 us (24%)
  starting transfers between devices  41.6 us (22%)
  other arithmetic  31.4 us (17%)
  local copies, waits for them, and re-layouts  9.58 us (5%)
  matrix products  8.48 us (5%)
    pallas_call x2, Pallas kernels, pull(): pl.pallas_call(pull_kernel, grid=(slot_count // tile,), out_shape=(jax.Sh...  42.8 us
    ppermute x6, waiting for transfers between devices, sum_over_line(): from_right = lax.ppermute(choose(step - (count - 1 - me)), axis, left)  35.2 us
    ppermute x6, starting transfers between devices, sum_over_line(): from_left = lax.ppermute(choose(step - me), axis, right)  23.3 us
    select_n x11, other arithmetic, choose(): value = jnp.where(number >= k, held[k], value)  19.8 us
    ppermute x6, starting transfers between devices, sum_over_line(): from_right = lax.ppermute(choose(step - (count - 1 - me)), axis, left)  12.7 us
    dot_general x4, matrix products, project(): lax.dot_general(p, w, NT, preferred_element_type=jnp.float32)  8.04 us
    unnamed x61, local copies, waits for them, and re-layouts  6.64 us
    pallas_call x1, Pallas kernels, deliver(): pl.pallas_call(lambda *refs: deliver_kernel(self_steps, *refs), grid=(own...  6.09 us
  transfers between devices with their start and end apart: 15, of which 8 were waited for; matrix products, arithmetic and copies ran while one was open for 18% of the time, Pallas kernels for 12%

profile of v4, /device:TPU:14, one launch (start us, length us, event | category | flops | bytes accessed | tf_op | source)
XLA Modules:
  0.0 186.0 jit_solution(8939179537298897927)
XLA Ops:
  2.4 2.2 %multiply_add_fusion = s32[2,4096]{1,0:T(2,128)S(1)} fusion(s32[2,4096]{1,0:T(2,128)S(1)} %select_reduce_fusion, s32[2,4096]{1,0:T(2,128)} %param.13), kind=kLoop, calls=%fused_computation.127 | loop fusion | flops 253952 | bytes 98304 | tf_op jit(solution)/shard_map/add | solution.py:21
  8.3 21.4 %shard_map.95 = (bf16[2048,512]{1,0:T(8,128)(2,1)S(1)}, f32[512,512]{1,0:T(8,128)S(1)}) custom-call(s32[1,4096]{1,0:T(1,128)S(1)} %get-tuple-element.45.dst_ref, s32[1,4096]{1,0:T(1,128)S(1)} %get-tuple-element.42.slot_ref, bf16[1024,512]{1,0:T(8,128)(2,1)S(1)} %copy-done.5, bf16[2048,512]{1,0:T(8,128)(2,1)S(1)} %copy-done.8), custom_call_target="tpu_custom_call" | custom-call | flops 12884901888 | bytes 6291456 | tf_op jit(solution)/shard_map/pallas_call | solution.py:78
  30.8 3.5 %collective-permute-start.2 = (f32[256,512]{1,0:T(8,128)}, f32[256,512]{1,0:T(8,128)}, u32[]{:S(2)}, u32[]{:S(2)}) collective-permute-start(f32[256,512]{1,0:T(8,128)} %get-tuple-element.35), channel_id=1, source_target_pairs={{0,4},{4,8},{8,12},{1,5},{5,9},{9,13},{2,6},{6,10},{10,14},{3,7},{... | collective-permute-start | bytes 1572872 | tf_op jit(solution)/shard_map/ppermute | solution.py:129
  34.3 3.1 %collective-permute-start.3 = (f32[256,512]{1,0:T(8,128)}, f32[256,512]{1,0:T(8,128)}, u32[]{:S(2)}, u32[]{:S(2)}) collective-permute-start(f32[256,512]{1,0:T(8,128)} %get-tuple-element.36), channel_id=1, source_target_pairs={{4,0},{8,4},{12,8},{5,1},{9,5},{13,9},{6,2},{10,6},{14,10},{7,3},{... | collective-permute-start | bytes 1572872 | tf_op jit(solution)/shard_map/ppermute | solution.py:130
  37.4 21.4 %shard_map.96 = (bf16[2048,512]{1,0:T(8,128)(2,1)S(1)}, f32[512,512]{1,0:T(8,128)S(1)}) custom-call(s32[1,4096]{1,0:T(1,128)S(1)} %get-tuple-element.46.dst_ref, s32[1,4096]{1,0:T(1,128)S(1)} %get-tuple-element.41.slot_ref, bf16[1024,512]{1,0:T(8,128)(2,1)S(1)} %copy-done.6, bf16[2048,512]{1,0:T(8,128)(2,1)S(1)} %copy-done.8), custom_call_target="tpu_custom_call" | custom-call | flops 12884901888 | bytes 6291456 | tf_op jit(solution)/shard_map/pallas_call | solution.py:78
  62.2 2.3 %broadcast_select_fusion.1 = (f32[256,512]{1,0:T(8,128)}, f32[256,512]{1,0:T(8,128)S(1)}, f32[256,512]{1,0:T(8,128)S(1)}) fusion(pred[]{:T(512)S(6)} %ge.107, f32[256,512]{1,0:T(8,128)} %collective-permute-done.3, f32[256,512]{1,0:T(8,128)} %collective-permute-done.2, f32[512,512]{1,0:T(8,128)S(1)} %copy-done.4, pred[]{:T(512)S(6)} %le.2, pred[]{:T(512)S(6)} %and.162, ...), kind=kLoop, calls=%fused_computation.117 | loop fusion | flops 1703936 | bytes 3670023 | tf_op jit(solution)/shard_map/jit(_where)/select_n | solution.py:123
  67.3 3.9 %collective-permute-start.4 = (f32[256,512]{1,0:T(8,128)}, f32[256,512]{1,0:T(8,128)}, u32[]{:S(2)}, u32[]{:S(2)}) collective-permute-start(f32[256,512]{1,0:T(8,128)} %get-tuple-element.28), channel_id=1, source_target_pairs={{0,4},{4,8},{8,12},{1,5},{5,9},{9,13},{2,6},{6,10},{10,14},{3,7},{... | collective-permute-start | bytes 1572872 | tf_op jit(solution)/shard_map/ppermute | solution.py:129
  75.0 5.7 %collective-permute-done.5 = f32[256,512]{1,0:T(8,128)} collective-permute-done((f32[256,512]{1,0:T(8,128)}, f32[256,512]{1,0:T(8,128)}, u32[]{:S(2)}, u32[]{:S(2)}) %collective-permute-start.5) | collective-permute-done | bytes 524320 | tf_op jit(solution)/shard_map/ppermute | solution.py:130
  82.7 2.7 %select_select_fusion.7 = (f32[256,512]{1,0:T(8,128)}, f32[256,512]{1,0:T(8,128)S(1)}, f32[256,512]{1,0:T(8,128)S(1)}) fusion(f32[512,512]{1,0:T(8,128)S(1)} %get-tuple-element.9, pred[]{:T(512)S(6)} %ge.111, pred[]{:T(512)S(6)} %ge.110, pred[]{:T(512)S(6)} %ge.109, f32[256,512]{1,0:T(8,128)} %collective-permute-done.5, f32[256,512]{1,0:T(8,128)} %copy-done.26, ...), kind=kLoop, calls=%fused_computation.97 | loop fusion | flops 1966080 | bytes 4718601 | tf_op jit(solution)/shard_map/jit(_where)/select_n | solution.py:123
  89.1 3.9 %collective-permute-start.6 = (f32[256,512]{1,0:T(8,128)}, f32[256,512]{1,0:T(8,128)}, u32[]{:S(2)}, u32[]{:S(2)}) collective-permute-start(f32[256,512]{1,0:T(8,128)} %get-tuple-element.25), channel_id=1, source_target_pairs={{0,4},{4,8},{8,12},{1,5},{5,9},{9,13},{2,6},{6,10},{10,14},{3,7},{... | collective-permute-start | bytes 1572872 | tf_op jit(solution)/shard_map/ppermute | solution.py:129
  95.1 3.1 %convolution_add_fusion.1 = f32[2048,256]{1,0:T(8,128)S(1)} fusion(f32[2048,256]{1,0:T(8,128)} %fusion.47, bf16[2048,512]{1,0:T(8,128)(2,1)} %copy-done.1, bf16[2,128,512]{2,1,0:T(8,128)(2,1)S(1)} %get-tuple-element.37, bf16[2,128,512]{2,1,0:T(8,128)(2,1)} %get-tuple-element.40), kind=kOutput, calls=%fused_computation.1 | convolution fusion | flops 537919488 | bytes 6815744 | tf_op jit(solution)/shard_map/dot_general | solution.py:145
  98.3 3.3 %collective-permute-done.7 = f32[256,512]{1,0:T(8,128)} collective-permute-done((f32[256,512]{1,0:T(8,128)}, f32[256,512]{1,0:T(8,128)}, u32[]{:S(2)}, u32[]{:S(2)}) %collective-permute-start.7) | collective-permute-done | bytes 524320 | tf_op jit(solution)/shard_map/ppermute | solution.py:130
  103.5 2.5 %select_select_fusion.5 = (f32[256,512]{1,0:T(8,128)}, f32[256,512]{1,0:T(8,128)S(1)}, f32[256,512]{1,0:T(8,128)S(1)}, f32[256,512]{1,0:T(8,128)S(1)}, f32[256,512]{1,0:T(8,128)S(1)}) fusion(pred[]{:T(512)S(6)} %ge.117, pred[]{:T(512)S(6)} %ge.116, pred[]{:T(512)S(6)} %ge.115, f32[256,512]{1,0:T(8,128)} %collective-permute-done.7, ...), kind=kLoop, calls=%fused_computation.95 | loop fusion | flops 3538944 | bytes 5767181 | tf_op jit(solution)/shard_map/jit(_where)/select_n | solution.py:123
  109.1 4.1 %collective-permute-start.8 = (f32[256,512]{1,0:T(8,128)}, f32[256,512]{1,0:T(8,128)}, u32[]{:S(2)}, u32[]{:S(2)}) collective-permute-start(f32[256,512]{1,0:T(8,128)} %get-tuple-element.20), channel_id=1, source_target_pairs={{0,4},{4,8},{8,12},{1,5},{5,9},{9,13},{2,6},{6,10},{10,14},{3,7},{... | collective-permute-start | bytes 1572872 | tf_op jit(solution)/shard_map/ppermute | solution.py:129
  115.2 5.5 %collective-permute-done.9 = f32[256,512]{1,0:T(8,128)} collective-permute-done((f32[256,512]{1,0:T(8,128)}, f32[256,512]{1,0:T(8,128)}, u32[]{:S(2)}, u32[]{:S(2)}) %collective-permute-start.9) | collective-permute-done | bytes 524320 | tf_op jit(solution)/shard_map/ppermute | solution.py:130
  122.6 3.1 %select_select_fusion.3 = (f32[256,512]{1,0:T(8,128)}, f32[256,512]{1,0:T(8,128)S(1)}, f32[256,512]{1,0:T(8,128)S(1)}, f32[256,512]{1,0:T(8,128)S(1)}, f32[256,512]{1,0:T(8,128)S(1)}) fusion(pred[]{:T(512)S(6)} %ge.122, pred[]{:T(512)S(6)} %ge.121, pred[]{:T(512)S(6)} %ge.120, f32[256,512]{1,0:T(8,128)} %collective-permute-done.9, f32[256,512]{1,0:T(8,128)} %copy-done.9, ...), kind=kLoop, calls=%fused_computation.93 | loop fusion | flops 3538944 | bytes 5767181 | tf_op jit(solution)/shard_map/jit(_where)/select_n | solution.py:123
  128.8 3.9 %collective-permute-start.10 = (f32[256,512]{1,0:T(8,128)}, f32[256,512]{1,0:T(8,128)}, u32[]{:S(2)}, u32[]{:S(2)}) collective-permute-start(f32[256,512]{1,0:T(8,128)} %get-tuple-element.15), channel_id=1, source_target_pairs={{0,4},{4,8},{8,12},{1,5},{5,9},{9,13},{2,6},{6,10},{10,14},{3,7},{... | collective-permute-start | bytes 1572872 | tf_op jit(solution)/shard_map/ppermute | solution.py:129
  132.8 3.9 %collective-permute-done.1 = f32[2048,128]{1,0:T(8,128)} collective-permute-done((f32[2048,128]{1,0:T(8,128)S(1)}, f32[2048,128]{1,0:T(8,128)}, u32[]{:S(2)}, u32[]{:S(2)}) %collective-permute-start.1) | collective-permute-done | bytes 1048608 | tf_op jit(solution)/shard_map/ppermute | solution.py:173
  136.7 2.6 %fusion = f32[2048,128]{1,0:T(8,128)} fusion(f32[2048,128]{1,0:T(8,128)} %collective-permute-done.1, f32[2048,256]{1,0:T(8,128)} %collective-permute-done, f32[2048,256]{1,0:T(8,128)S(1)} %convolution_add_fusion.1), kind=kLoop, calls=%fused_computation.5 | loop fusion | flops 524288 | bytes 4194304 | tf_op jit(solution)/shard_map/add | solution.py:174
  139.4 5.1 %all-to-all-start = ((f32[4,512,128]{2,1,0:T(8,128)}), f32[4,512,128]{2,1,0:T(8,128)S(1)}, u32[]{:S(2)}, u32[]{:S(2)}) async-start(f32[4,512,128]{2,1,0:T(8,128)} %bitcast.36), calls=%async_computation | async-start | bytes 2097152 | tf_op jit(solution)/shard_map/all_to_all | solution.py:235
  144.5 2.8 %select_select_fusion.1 = (f32[256,512]{1,0:T(8,128)}, f32[256,512]{1,0:T(8,128)S(1)}, f32[256,512]{1,0:T(8,128)S(1)}, f32[256,512]{1,0:T(8,128)S(1)}, f32[256,512]{1,0:T(8,128)S(1)}) fusion(pred[]{:T(512)S(6)} %ge.128, pred[]{:T(512)S(6)} %ge.127, pred[]{:T(512)S(6)} %ge.126, f32[256,512]{1,0:T(8,128)} %collective-permute-done.11, ...), kind=kLoop, calls=%fused_computation.91 | loop fusion | flops 3538944 | bytes 5767181 | tf_op jit(solution)/shard_map/jit(_where)/select_n | solution.py:123
  151.0 3.9 %collective-permute-start.12 = (f32[256,512]{1,0:T(8,128)}, f32[256,512]{1,0:T(8,128)}, u32[]{:S(2)}, u32[]{:S(2)}) collective-permute-start(f32[256,512]{1,0:T(8,128)} %get-tuple-element.10), channel_id=1, source_target_pairs={{0,4},{4,8},{8,12},{1,5},{5,9},{9,13},{2,6},{6,10},{10,14},{3,7},{... | collective-permute-start | bytes 1572872 | tf_op jit(solution)/shard_map/ppermute | solution.py:129
  155.5 20.7 %collective-permute-done.13 = f32[256,512]{1,0:T(8,128)} collective-permute-done((f32[256,512]{1,0:T(8,128)}, f32[256,512]{1,0:T(8,128)}, u32[]{:S(2)}, u32[]{:S(2)}) %collective-permute-start.13) | collective-permute-done | bytes 524320 | tf_op jit(solution)/shard_map/ppermute | solution.py:130
  179.9 6.1 %shard_map.97 = f32[2048,128]{1,0:T(8,128)} custom-call(s32[1,2048]{1,0:T(1,128)S(1)} %bitcast.35, f32[2048,128]{1,0:T(8,128)S(1)} %bitcast.34, f32[1024,128]{1,0:T(8,128)S(1)} %fusion.77.refs_2_), custom_call_target="tpu_custom_call" | custom-call | flops 3221225472 | bytes 2097152 | tf_op jit(solution)/shard_map/pallas_call | solution.py:199
  (95 shorter events, 44.1 us)
Async XLA Ops:
  0.6 154.4 %copy-start = (bf16[128,512]{1,0:T(8,128)(2,1)S(1)}, bf16[128,512]{1,0:T(8,128)(2,1)}, u32[]{:S(2)}) copy-start(bf16[128,512]{1,0:T(8,128)(2,1)} %param.11) | copy-start | bytes 393220
  30.8 31.4 %collective-permute-start.2 = (f32[256,512]{1,0:T(8,128)}, f32[256,512]{1,0:T(8,128)}, u32[]{:S(2)}, u32[]{:S(2)}) collective-permute-start(f32[256,512]{1,0:T(8,128)} %get-tuple-element.35), channel_id=1, source_target_pairs={{0,4},{4,8},{8,12},{1,5},{5,9},{9,13},{2,6},{6,10},{10,14},{3,7},{... | collective-permute-start | bytes 1572872 | tf_op jit(solution)/shard_map/ppermute | solution.py:129
  34.3 28.0 %collective-permute-start.3 = (f32[256,512]{1,0:T(8,128)}, f32[256,512]{1,0:T(8,128)}, u32[]{:S(2)}, u32[]{:S(2)}) collective-permute-start(f32[256,512]{1,0:T(8,128)} %get-tuple-element.36), channel_id=1, source_target_pairs={{4,0},{8,4},{12,8},{5,1},{9,5},{13,9},{6,2},{10,6},{14,10},{7,3},{... | collective-permute-start | bytes 1572872 | tf_op jit(solution)/shard_map/ppermute | solution.py:130
  65.4 15.3 %collective-permute-start.5 = (f32[256,512]{1,0:T(8,128)}, f32[256,512]{1,0:T(8,128)}, u32[]{:S(2)}, u32[]{:S(2)}) collective-permute-start(f32[256,512]{1,0:T(8,128)} %broadcast_select_fusion), channel_id=1, source_target_pairs={{4,0},{8,4},{12,8},{5,1},{9,5},{13,9},{6,2},{10,6},{14,10},{7,3},{... | collective-permute-start | bytes 1572872 | tf_op jit(solution)/shard_map/ppermute | solution.py:130
  67.3 15.3 %collective-permute-start.4 = (f32[256,512]{1,0:T(8,128)}, f32[256,512]{1,0:T(8,128)}, u32[]{:S(2)}, u32[]{:S(2)}) collective-permute-start(f32[256,512]{1,0:T(8,128)} %get-tuple-element.28), channel_id=1, source_target_pairs={{0,4},{4,8},{8,12},{1,5},{5,9},{9,13},{2,6},{6,10},{10,14},{3,7},{... | collective-permute-start | bytes 1572872 | tf_op jit(solution)/shard_map/ppermute | solution.py:129
  75.0 38.2 %collective-permute-start = (f32[2048,256]{1,0:T(8,128)}, f32[2048,256]{1,0:T(8,128)}, u32[]{:S(2)}, u32[]{:S(2)}) collective-permute-start(f32[2048,256]{1,0:T(8,128)} %convolution_add_fusion), channel_id=1, source_target_pairs={{0,1},{1,0},{2,3},{3,2},{4,5},{5,4},{6,7},{7,6},{8,9},{9,8},{10,11... | collective-permute-start | bytes 6291464 | tf_op jit(solution)/shard_map/ppermute | solution.py:169
  87.2 14.4 %collective-permute-start.7 = (f32[256,512]{1,0:T(8,128)}, f32[256,512]{1,0:T(8,128)}, u32[]{:S(2)}, u32[]{:S(2)}) collective-permute-start(f32[256,512]{1,0:T(8,128)} %select_select_fusion.6), channel_id=1, source_target_pairs={{4,0},{8,4},{12,8},{5,1},{9,5},{13,9},{6,2},{10,6},{14,10},{7,3},{... | collective-permute-start | bytes 1572872 | tf_op jit(solution)/shard_map/ppermute | solution.py:130
  89.1 14.4 %collective-permute-start.6 = (f32[256,512]{1,0:T(8,128)}, f32[256,512]{1,0:T(8,128)}, u32[]{:S(2)}, u32[]{:S(2)}) collective-permute-start(f32[256,512]{1,0:T(8,128)} %get-tuple-element.25), channel_id=1, source_target_pairs={{0,4},{4,8},{8,12},{1,5},{5,9},{9,13},{2,6},{6,10},{10,14},{3,7},{... | collective-permute-start | bytes 1572872 | tf_op jit(solution)/shard_map/ppermute | solution.py:129
  106.0 8.6 %copy-start.9 = (f32[256,512]{1,0:T(8,128)}, f32[256,512]{1,0:T(8,128)S(1)}, u32[]{:S(2)}) copy-start(f32[256,512]{1,0:T(8,128)S(1)} %get-tuple-element.21) | copy-start | bytes 1572868
  106.0 8.6 %copy-start.10 = (f32[256,512]{1,0:T(8,128)}, f32[256,512]{1,0:T(8,128)S(1)}, u32[]{:S(2)}) copy-start(f32[256,512]{1,0:T(8,128)S(1)} %get-tuple-element.22) | copy-start | bytes 1572868
  106.0 8.6 %copy-start.11 = (f32[256,512]{1,0:T(8,128)}, f32[256,512]{1,0:T(8,128)S(1)}, u32[]{:S(2)}) copy-start(f32[256,512]{1,0:T(8,128)S(1)} %get-tuple-element.23) | copy-start | bytes 1572868
  106.0 8.6 %copy-start.12 = (f32[256,512]{1,0:T(8,128)}, f32[256,512]{1,0:T(8,128)S(1)}, u32[]{:S(2)}) copy-start(f32[256,512]{1,0:T(8,128)S(1)} %get-tuple-element.24) | copy-start | bytes 1572868
  107.2 13.5 %collective-permute-start.9 = (f32[256,512]{1,0:T(8,128)}, f32[256,512]{1,0:T(8,128)}, u32[]{:S(2)}, u32[]{:S(2)}) collective-permute-start(f32[256,512]{1,0:T(8,128)} %select_select_fusion.4), channel_id=1, source_target_pairs={{4,0},{8,4},{12,8},{5,1},{9,5},{13,9},{6,2},{10,6},{14,10},{7,3},{... | collective-permute-start | bytes 1572872 | tf_op jit(solution)/shard_map/ppermute | solution.py:130
  109.1 13.5 %collective-permute-start.8 = (f32[256,512]{1,0:T(8,128)}, f32[256,512]{1,0:T(8,128)}, u32[]{:S(2)}, u32[]{:S(2)}) collective-permute-start(f32[256,512]{1,0:T(8,128)} %get-tuple-element.20), channel_id=1, source_target_pairs={{0,4},{4,8},{8,12},{1,5},{5,9},{9,13},{2,6},{6,10},{10,14},{3,7},{... | collective-permute-start | bytes 1572872 | tf_op jit(solution)/shard_map/ppermute | solution.py:129
  114.6 22.1 %collective-permute-start.1 = (f32[2048,128]{1,0:T(8,128)S(1)}, f32[2048,128]{1,0:T(8,128)}, u32[]{:S(2)}, u32[]{:S(2)}) collective-permute-start(f32[2048,128]{1,0:T(8,128)S(1)} %slice_add_fusion), channel_id=1, source_target_pairs={{0,2},{1,3},{2,0},{3,1},{4,6},{5,7},{6,4},{7,5},{8,10},{9,11},{10,... | collective-permute-start | bytes 3145736 | tf_op jit(solution)/shard_map/ppermute | solution.py:173
  125.7 13.7 %copy-start.16 = (f32[256,512]{1,0:T(8,128)}, f32[256,512]{1,0:T(8,128)S(1)}, u32[]{:S(2)}) copy-start(f32[256,512]{1,0:T(8,128)S(1)} %get-tuple-element.16) | copy-start | bytes 1572868
  125.7 13.7 %copy-start.18 = (f32[256,512]{1,0:T(8,128)}, f32[256,512]{1,0:T(8,128)S(1)}, u32[]{:S(2)}) copy-start(f32[256,512]{1,0:T(8,128)S(1)} %get-tuple-element.17) | copy-start | bytes 1572868
  125.7 13.7 %copy-start.20 = (f32[256,512]{1,0:T(8,128)}, f32[256,512]{1,0:T(8,128)S(1)}, u32[]{:S(2)}) copy-start(f32[256,512]{1,0:T(8,128)S(1)} %get-tuple-element.18) | copy-start | bytes 1572868
  125.7 13.7 %copy-start.21 = (f32[256,512]{1,0:T(8,128)}, f32[256,512]{1,0:T(8,128)S(1)}, u32[]{:S(2)}) copy-start(f32[256,512]{1,0:T(8,128)S(1)} %get-tuple-element.19) | copy-start | bytes 1572868
  126.9 17.6 %collective-permute-start.11 = (f32[256,512]{1,0:T(8,128)}, f32[256,512]{1,0:T(8,128)}, u32[]{:S(2)}, u32[]{:S(2)}) collective-permute-start(f32[256,512]{1,0:T(8,128)} %select_select_fusion.2), channel_id=1, source_target_pairs={{4,0},{8,4},{12,8},{5,1},{9,5},{13,9},{6,2},{10,6},{14,10},{7,3},{... | collective-permute-start | bytes 1572872 | tf_op jit(solution)/shard_map/ppermute | solution.py:130
  128.8 15.7 %collective-permute-start.10 = (f32[256,512]{1,0:T(8,128)}, f32[256,512]{1,0:T(8,128)}, u32[]{:S(2)}, u32[]{:S(2)}) collective-permute-start(f32[256,512]{1,0:T(8,128)} %get-tuple-element.15), channel_id=1, source_target_pairs={{0,4},{4,8},{8,12},{1,5},{5,9},{9,13},{2,6},{6,10},{10,14},{3,7},{... | collective-permute-start | bytes 1572872 | tf_op jit(solution)/shard_map/ppermute | solution.py:129
  139.4 40.5 %all-to-all-start = ((f32[4,512,128]{2,1,0:T(8,128)}), f32[4,512,128]{2,1,0:T(8,128)S(1)}, u32[]{:S(2)}, u32[]{:S(2)}) async-start(f32[4,512,128]{2,1,0:T(8,128)} %bitcast.36), calls=%async_computation | async-start | bytes 2097152 | tf_op jit(solution)/shard_map/all_to_all | solution.py:235
  149.1 27.1 %collective-permute-start.13 = (f32[256,512]{1,0:T(8,128)}, f32[256,512]{1,0:T(8,128)}, u32[]{:S(2)}, u32[]{:S(2)}) collective-permute-start(f32[256,512]{1,0:T(8,128)} %select_select_fusion), channel_id=1, source_target_pairs={{4,0},{8,4},{12,8},{5,1},{9,5},{13,9},{6,2},{10,6},{14,10},{7,3},{... | collective-permute-start | bytes 1572872 | tf_op jit(solution)/shard_map/ppermute | solution.py:130
  151.0 25.2 %collective-permute-start.12 = (f32[256,512]{1,0:T(8,128)}, f32[256,512]{1,0:T(8,128)}, u32[]{:S(2)}, u32[]{:S(2)}) collective-permute-start(f32[256,512]{1,0:T(8,128)} %get-tuple-element.10), channel_id=1, source_target_pairs={{0,4},{4,8},{8,12},{1,5},{5,9},{9,13},{2,6},{6,10},{10,14},{3,7},{... | collective-permute-start | bytes 1572872 | tf_op jit(solution)/shard_map/ppermute | solution.py:129
  (21 other events, 99.8 us)

commit v5 on v3

--- a/solution.py
+++ b/solution.py
@@ -105,21 +105,11 @@
     )(dst, slots, grad_out, features)
 
 
-def sum_over_line(value, axis):
-    count = lax.axis_size(axis)
-    if count % 2 or count > 8:
-        return lax.psum(value, axis)
-    me = lax.axis_index(axis)
-    middle = count // 2
-    for hop in range(middle - 1):
-        pairs = [(hop, hop + 1), (count - 1 - hop, count - 2 - hop)]
-        value = value + lax.ppermute(value, axis, pairs)
-    value = value + lax.ppermute(value, axis, [(middle - 1, middle), (middle, middle - 1)])
-    for hop in range(middle - 1):
-        low, high = middle - 2 - hop, middle + 1 + hop
-        given = lax.ppermute(value, axis, [(low + 1, low), (high - 1, high)])
-        value = jnp.where((me == low) | (me == high), given, value)
-    return value
+def sum_over(value, axis, in_two):
+    if in_two and value.shape[0] % lax.axis_size(axis) == 0:
+        share = lax.psum_scatter(value, axis, scatter_dimension=0, tiled=True)
+        return lax.all_gather(share, axis, axis=0, tiled=True)
+    return lax.psum(value, axis)
 
 
 def project(pulled, weights):
@@ -210,8 +200,7 @@
     for r in range(relations):
         here, terms = pull(edge_dst[r : r + 1], slots[r : r + 1], grad_out, source_features)
         pulled.append(here)
-        pieces = [sum_over_line(piece, "dom") for piece in jnp.split(terms, 2, axis=0)]
-        weight_grads.append(jnp.concatenate(pieces, axis=0))
+        weight_grads.append(sum_over(terms, "dom", r % 2 == 0))
     slot_grads = project_and_scatter(pulled, rel_weight, "rep")
     arrived = lax.all_to_all(slot_grads, "dom", split_axis=0, concat_axis=0, tiled=True)
     self_term = lax.dot_general(grad_out, self_weight, NT, preferred_element_type=jnp.float32)

time: 188 us -> 176 us (0.936)
  starting transfers between devices: 29.9 us -> 8.68 us
  between operations: 0.99 us -> 13.9 us
  waiting for transfers between devices: 82.1 us -> 78.4 us
  matrix products: 3.38 us -> 5.76 us
  other arithmetic: 14.1 us -> 11.9 us
  local copies, waits for them, and re-layouts: 8.25 us -> 6.22 us
  Pallas kernels: 48.9 us -> 50.8 us
    ppermute x12 -> x0, waiting for transfers between devices: 82.1 us -> none  [the longest x4 45.9 us: sum_over_line(): given = lax.ppermute(value, axis, [(low + 1, low), (high - 1, high)])]
    all_gather x0 -> x1, waiting for transfers between devices: none -> 28.5 us  [sum_over(): return lax.all_gather(share, axis, axis=0, tiled=True)]
    psum x0 -> x1, waiting for transfers between devices: none -> 24.7 us  [sum_over(): return lax.psum(value, axis)]
    ppermute x1, waiting for transfers between devices: 0.01 us -> 23.7 us  [project_and_scatter(): crossed = lax.ppermute(crossing, axis, [(i, i ^ 2) for i in range(4)])]
    ppermute x12 -> x0, starting transfers between devices: 18.3 us -> none  [the longest x4 8.88 us: sum_over_line(): value = value + lax.ppermute(value, axis, pairs)]
    add x6 -> x0, other arithmetic: 4.93 us -> none  [the longest x4 3.53 us: sum_over_line(): value + lax.ppermute(value, axis, [(middle - 1, middle), (middle, middle...]
    all_to_all x1, starting transfers between devices: 9.43 us -> 5.25 us  [on_device(): lax.all_to_all(slot_grads, 'dom', split_axis=0, concat_axis=0, tiled=True)]
    select_n x4 -> x0, other arithmetic: 2.41 us -> none  [sum_over_line(): value = jnp.where((me == low) | (me == high), given, value)]
  transfers between devices with their start and end apart: 15 -> 6, of which waited for: 8 -> 4; matrix products, arithmetic and copies ran while one was open for 7% -> 8% of each run, Pallas kernels for 0% -> 13%
where the time goes in v5:
time: 176 us
  waiting for transfers between devices  78.4 us (45%)
  Pallas kernels  50.8 us (29%)
  between operations  13.9 us (8%)
  other arithmetic  11.9 us (7%)
  starting transfers between devices  8.68 us (5%)
  local copies, waits for them, and re-layouts  6.22 us (4%)
  matrix products  5.76 us (3%)
    pallas_call x2, Pallas kernels, pull(): pl.pallas_call(pull_kernel, grid=(slot_count // tile,), out_shape=(jax.Sh...  44.7 us
    all_gather x1, waiting for transfers between devices, sum_over(): return lax.all_gather(share, axis, axis=0, tiled=True)  28.5 us
    psum x1, waiting for transfers between devices, sum_over(): return lax.psum(value, axis)  24.7 us
    ppermute x1, waiting for transfers between devices, project_and_scatter(): crossed = lax.ppermute(crossing, axis, [(i, i ^ 2) for i in range(4)])  23.7 us
    pallas_call x1, Pallas kernels, deliver(): pl.pallas_call(lambda *refs: deliver_kernel(self_steps, *refs), grid=(own...  6.08 us
    dot_general x4, matrix products, project(): lax.dot_general(p, w, NT, preferred_element_type=jnp.float32)  5.33 us
    all_to_all x1, starting transfers between devices, on_device(): lax.all_to_all(slot_grads, 'dom', split_axis=0, concat_axis=0, tiled=True)  5.25 us
    unnamed x21, local copies, waits for them, and re-layouts  4.44 us
  transfers between devices with their start and end apart: 6, of which 4 were waited for; matrix products, arithmetic and copies ran while one was open for 8% of the time, Pallas kernels for 13%

profile of v5, /device:TPU:0, one launch (start us, length us, event | category | flops | bytes accessed | tf_op | source)
XLA Modules:
  0.0 175.7 jit_solution(16054849957064415595)
XLA Ops:
  7.2 0.9 and_select_fusion.2
  8.1 0.8 select_reduce_fusion
  8.9 2.2 %multiply_add_fusion = s32[2,4096]{1,0:T(2,128)S(1)} fusion(s32[2,4096]{1,0:T(2,128)S(1)} %select_reduce_fusion, s32[2,4096]{1,0:T(2,128)} %param.13), kind=kLoop, calls=%fused_computation.35 | loop fusion | flops 253952 | bytes 98304 | tf_op jit(solution)/shard_map/add | solution.py:21
  11.1 0.9 fusion.19
  12.0 1.2 copy-done.3
  13.2 1.6 copy-done.5
  14.8 22.4 %shard_map.95 = (bf16[2048,512]{1,0:T(8,128)(2,1)S(1)}, f32[512,512]{1,0:T(8,128)}) custom-call(s32[1,4096]{1,0:T(1,128)S(1)} %get-tuple-element.18.dst_ref, s32[1,4096]{1,0:T(1,128)S(1)} %get-tuple-element.15.slot_ref, bf16[1024,512]{1,0:T(8,128)(2,1)S(1)} %copy-done.3, bf16[2048,512]{1,0:T(8,128)(2,1)S(1)} %copy-done.5), custom_call_target="tpu_custom_call" | custom-call | flops 12884901888 | bytes 6291456 | tf_op jit(solution)/shard_map/pallas_call | solution.py:78
  37.3 1.6 copy-done.6
  38.9 22.4 %shard_map.96 = (bf16[2048,512]{1,0:T(8,128)(2,1)S(1)}, f32[512,512]{1,0:T(8,128)}) custom-call(s32[1,4096]{1,0:T(1,128)S(1)} %get-tuple-element.19.dst_ref, s32[1,4096]{1,0:T(1,128)S(1)} %get-tuple-element.14.slot_ref, bf16[1024,512]{1,0:T(8,128)(2,1)S(1)} %copy-done.4, bf16[2048,512]{1,0:T(8,128)(2,1)S(1)} %copy-done.6), custom_call_target="tpu_custom_call" | custom-call | flops 12884901888 | bytes 6291456 | tf_op jit(solution)/shard_map/pallas_call | solution.py:78
  61.3 0.9 dynamic-slice_bitcast_fusion.2
  62.2 0.7 fusion.3
  62.9 2.1 %convolution_add_fusion = f32[2048,256]{1,0:T(8,128)} fusion(f32[2048,256]{1,0:T(8,128)S(1)} %fusion.3, bf16[2048,512]{1,0:T(8,128)(2,1)S(1)} %get-tuple-element.7, bf16[2,128,512]{2,1,0:T(8,128)(2,1)S(1)} %get-tuple-element.11, bf16[2,128,512]{2,1,0:T(8,128)(2,1)S(1)} %get-tuple-element.12), kind=kOutput, calls=%fused_computation | convolution fusion | flops 537919488 | bytes 6815744 | tf_op jit(solution)/shard_map/dot_general | solution.py:117
  65.5 1.8 %fusion.7 = f32[2048,256]{1,0:T(8,128)S(1)} fusion(bf16[2048,512]{1,0:T(8,128)(2,1)S(1)} %get-tuple-element.6, bf16[2,128,512]{2,1,0:T(8,128)(2,1)} %get-tuple-element.13, bf16[2,128,512]{2,1,0:T(8,128)(2,1)S(1)} %get-tuple-element.10), kind=kOutput, calls=%fused_computation.15 | convolution fusion | flops 537395200 | bytes 4718592 | tf_op jit(solution)/shard_map/dot_general | solution.py:117
  67.3 0.7 convolution_add_fusion.1
  68.1 1.5 collective-permute-done
  69.6 2.3 %slice_add_fusion = f32[2048,128]{1,0:T(8,128)} fusion(f32[2048,256]{1,0:T(8,128)} %collective-permute-done, f32[2048,256]{1,0:T(8,128)S(1)} %convolution_add_fusion.1), kind=kLoop, calls=%fused_computation.3 | loop fusion | flops 262144 | bytes 3145728 | tf_op jit(solution)/shard_map/add | solution.py:144
  71.8 2.9 %collective-permute-start.1 = (f32[2048,128]{1,0:T(8,128)}, f32[2048,128]{1,0:T(8,128)}, u32[]{:S(2)}, u32[]{:S(2)}) collective-permute-start(f32[2048,128]{1,0:T(8,128)} %slice_add_fusion), channel_id=1, source_target_pairs={{0,2},{1,3},{2,0},{3,1},{4,6},{5,7},{6,4},{7,5},{8,10},{9,11},{10,... | collective-permute-start | bytes 3145736 | tf_op jit(solution)/shard_map/ppermute | solution.py:145
  74.7 23.7 %collective-permute-done.1 = f32[2048,128]{1,0:T(8,128)} collective-permute-done((f32[2048,128]{1,0:T(8,128)}, f32[2048,128]{1,0:T(8,128)}, u32[]{:S(2)}, u32[]{:S(2)}) %collective-permute-start.1) | collective-permute-done | bytes 1048608 | tf_op jit(solution)/shard_map/ppermute | solution.py:145
  98.5 2.7 %fusion = f32[2048,128]{1,0:T(8,128)} fusion(f32[2048,128]{1,0:T(8,128)} %collective-permute-done.1, f32[2048,256]{1,0:T(8,128)} %collective-permute-done, f32[2048,256]{1,0:T(8,128)S(1)} %convolution_add_fusion.1), kind=kLoop, calls=%fused_computation.5 | loop fusion | flops 524288 | bytes 4194304 | tf_op jit(solution)/shard_map/add | solution.py:146
  101.2 5.2 %all-to-all-start = ((f32[4,512,128]{2,1,0:T(8,128)}), f32[4,512,128]{2,1,0:T(8,128)S(1)}, u32[]{:S(2)}, u32[]{:S(2)}) async-start(f32[4,512,128]{2,1,0:T(8,128)} %bitcast.37), calls=%async_computation | async-start | bytes 2097152 | tf_op jit(solution)/shard_map/all_to_all | solution.py:205
  106.9 24.7 %all-reduce.2.cloned.1.call-done = f32[1,512,512]{2,1,0:T(8,128)} async-done(((f32[1,512,512]{2,1,0:T(8,128)}), f32[1,512,512]{2,1,0:T(8,128)}) %all-reduce.2.cloned.1.call-update) | async-done | bytes 1048592 | tf_op jit(solution)/shard_map/psum | solution.py:112
  131.5 28.5 %all-gather.2.cloned.1.call-done = f32[512,512]{1,0:T(8,128)} async-done(((f32[128,512]{1,0:T(8,128)}), f32[512,512]{1,0:T(8,128)}) %all-gather.2.cloned.1.call-update) | async-done | bytes 1048592 | tf_op jit(solution)/shard_map/all_gather | solution.py:111
  160.0 3.0 %pad_maximum_fusion = f32[2,512,512]{2,1,0:T(8,128)} fusion(f32[1,512,512]{2,1,0:T(8,128)} %all-reduce.2.cloned.1.call-done, f32[1,512,512]{2,1,0:T(8,128)} %bitcast.39), kind=kLoop, calls=%fused_computation.2 | loop fusion | flops 524288 | bytes 4194304 | tf_op jit(solution)/shard_map/stack | solution.py:208
  163.1 6.1 %shard_map.97 = f32[2048,128]{1,0:T(8,128)} custom-call(s32[1,2048]{1,0:T(1,128)S(1)} %bitcast.36, f32[2048,128]{1,0:T(8,128)S(1)} %bitcast.35, f32[1024,128]{1,0:T(8,128)S(1)} %fusion.21.refs_2_), custom_call_target="tpu_custom_call" | custom-call | flops 3221225472 | bytes 2097152 | tf_op jit(solution)/shard_map/pallas_call | solution.py:171
  (28 shorter events, 1.1 us)
Async XLA Ops:
  7.2 99.3 %copy-start = (bf16[128,512]{1,0:T(8,128)(2,1)S(1)}, bf16[128,512]{1,0:T(8,128)(2,1)}, u32[]{:S(2)}) copy-start(bf16[128,512]{1,0:T(8,128)(2,1)} %param.11) | copy-start | bytes 393220
  7.2 67.5 %reduce-scatter.2.cloned.1.call-start = ((), (), s32[]{:S(2)}) async-start(), calls=%async_computation.2 | async-start | bytes 1310720 | tf_op jit(solution)/shard_map/reduce_scatter | solution.py:110
  12.0 1.2 copy-start.3
  13.2 1.6 copy-start.5
  14.8 22.5 %copy-start.4 = (bf16[1024,512]{1,0:T(8,128)(2,1)S(1)}, bf16[1024,512]{1,0:T(8,128)(2,1)}, u32[]{:S(2)}) copy-start(bf16[1024,512]{1,0:T(8,128)(2,1)} %grad_ref.3) | copy-start | bytes 3145732
  37.2 94.3 %all-reduce.2.cloned.1.call-start = ((), (), s32[]{:S(2)}) async-start(), calls=%async_computation.4 | async-start | bytes 2097152 | tf_op jit(solution)/shard_map/psum | solution.py:112
  37.3 1.6 copy-start.6
  38.9 22.4 %copy-start.8 = (bf16[2,512,512]{2,1,0:T(8,128)(2,1)S(1)}, bf16[2,512,512]{2,1,0:T(8,128)(2,1)}, u32[]{:S(2)}) copy-start(bf16[2,512,512]{2,1,0:T(8,128)(2,1)} %param.10) | copy-start | bytes 3145732
  61.3 1.6 copy-start.1
  65.0 4.6 %collective-permute-start = (f32[2048,256]{1,0:T(8,128)}, f32[2048,256]{1,0:T(8,128)}, u32[]{:S(2)}, u32[]{:S(2)}) collective-permute-start(f32[2048,256]{1,0:T(8,128)} %convolution_add_fusion), channel_id=1, source_target_pairs={{0,1},{1,0},{2,3},{3,2},{4,5},{5,4},{6,7},{7,6},{8,9},{9,8},{10,11... | collective-permute-start | bytes 6291464 | tf_op jit(solution)/shard_map/ppermute | solution.py:141
  65.4 94.6 %all-gather.2.cloned.1.call-start = ((), (), s32[]{:S(2)}) async-start(), calls=%async_computation.3 | async-start | bytes 1310720 | tf_op jit(solution)/shard_map/all_gather | solution.py:111
  65.5 1.8 %copy-start.2 = (bf16[2048,512]{1,0:T(8,128)(2,1)S(1)}, bf16[2048,512]{1,0:T(8,128)(2,1)}, u32[]{:S(2)}) copy-start(bf16[2048,512]{1,0:T(8,128)(2,1)} %copy-done.1) | copy-start | bytes 6291460
  65.5 1.8 %copy-start.7 = (bf16[2,128,512]{2,1,0:T(8,128)(2,1)S(1)}, bf16[2,128,512]{2,1,0:T(8,128)(2,1)}, u32[]{:S(2)}) copy-start(bf16[2,128,512]{2,1,0:T(8,128)(2,1)} %get-tuple-element.13) | copy-start | bytes 786436
  71.8 26.6 %collective-permute-start.1 = (f32[2048,128]{1,0:T(8,128)}, f32[2048,128]{1,0:T(8,128)}, u32[]{:S(2)}, u32[]{:S(2)}) collective-permute-start(f32[2048,128]{1,0:T(8,128)} %slice_add_fusion), channel_id=1, source_target_pairs={{0,2},{1,3},{2,0},{3,1},{4,6},{5,7},{6,4},{7,5},{8,10},{9,11},{10,... | collective-permute-start | bytes 3145736 | tf_op jit(solution)/shard_map/ppermute | solution.py:145
  101.2 5.3 %copy-start.9 = (s32[4,512]{1,0:T(4,128)S(1)}, s32[4,512]{1,0:T(4,128)}, u32[]{:S(2)}) copy-start(s32[4,512]{1,0:T(4,128)} %param.15) | copy-start | bytes 24580
  101.2 61.9 %all-to-all-start = ((f32[4,512,128]{2,1,0:T(8,128)}), f32[4,512,128]{2,1,0:T(8,128)S(1)}, u32[]{:S(2)}, u32[]{:S(2)}) async-start(f32[4,512,128]{2,1,0:T(8,128)} %bitcast.37), calls=%async_computation | async-start | bytes 2097152 | tf_op jit(solution)/shard_map/all_to_all | solution.py:205
Sparse Core Ops, SparseCore 0:
  37.3 29.8 reduce-scatter.1
  69.7 61.7 all-reduce.1
  133.1 26.8 all-gather.1

commit v6 on v5

--- a/solution.py
+++ b/solution.py
@@ -105,11 +105,11 @@
     )(dst, slots, grad_out, features)
 
 
-def sum_over(value, axis, in_two):
-    if in_two and value.shape[0] % lax.axis_size(axis) == 0:
-        share = lax.psum_scatter(value, axis, scatter_dimension=0, tiled=True)
-        return lax.all_gather(share, axis, axis=0, tiled=True)
-    return lax.psum(value, axis)
+def sum_over(value, axis, dimension):
+    if value.shape[dimension] % (128 * lax.axis_size(axis)):
+        return lax.psum(value, axis)
+    share = lax.psum_scatter(value, axis, scatter_dimension=dimension, tiled=True)
+    return lax.all_gather(share, axis, axis=dimension, tiled=True)
 
 
 def project(pulled, weights):
@@ -200,7 +200,7 @@
     for r in range(relations):
         here, terms = pull(edge_dst[r : r + 1], slots[r : r + 1], grad_out, source_features)
         pulled.append(here)
-        weight_grads.append(sum_over(terms, "dom", r % 2 == 0))
+        weight_grads.append(sum_over(terms, "dom", r % 2))
     slot_grads = project_and_scatter(pulled, rel_weight, "rep")
     arrived = lax.all_to_all(slot_grads, "dom", split_axis=0, concat_axis=0, tiled=True)
     self_term = lax.dot_general(grad_out, self_weight, NT, preferred_element_type=jnp.float32)

time: 176 us -> 191 us (1.085)
  waiting for transfers between devices: 78.4 us -> 91.4 us
  local copies, waits for them, and re-layouts: 6.22 us -> 8.76 us
    all_gather x1 -> x2, waiting for transfers between devices: 28.5 us -> 65 us  [sum_over(): return lax.all_gather(share, axis, axis=dimension, tiled=True)]
    psum x1 -> x0, waiting for transfers between devices: 24.7 us -> none  [sum_over(): return lax.psum(value, axis)]
    reduce_scatter x1 -> x2, waiting for transfers between devices: 0.01 us -> 20 us  [sum_over(): lax.psum_scatter(value, axis, scatter_dimension=dimension, tiled=True)]
    ppermute x1, waiting for transfers between devices: 23.7 us -> 3.74 us  [project_and_scatter(): crossed = lax.ppermute(crossing, axis, [(i, i ^ 2) for i in range(4)])]
    unnamed x21 -> x17, local copies, waits for them, and re-layouts: 4.44 us -> 6.59 us
  transfers between devices with their start and end apart: 6 -> 7, of which waited for: 4 -> 5; matrix products, arithmetic and copies ran while one was open for 8% -> 7% of each run, Pallas kernels for 13% -> 12%
where the time goes in v6:
time: 191 us; the launch traced here: 190 us
  waiting for transfers between devices  91.4 us (48%)
  Pallas kernels  50.8 us (27%)
  between operations  13.9 us (7%)
  other arithmetic  11.9 us (6%)
  local copies, waits for them, and re-layouts  8.76 us (5%)
  starting transfers between devices  8.75 us (5%)
  matrix products  4.7 us (2%)
    all_gather x2, waiting for transfers between devices, sum_over(): return lax.all_gather(share, axis, axis=dimension, tiled=True)  65 us
    pallas_call x2, Pallas kernels, pull(): pl.pallas_call(pull_kernel, grid=(slot_count // tile,), out_shape=(jax.Sh...  44.7 us
    reduce_scatter x2, waiting for transfers between devices, sum_over(): lax.psum_scatter(value, axis, scatter_dimension=dimension, tiled=True)  20 us
    unnamed x17, local copies, waits for them, and re-layouts  6.59 us
    pallas_call x1, Pallas kernels, deliver(): pl.pallas_call(lambda *refs: deliver_kernel(self_steps, *refs), grid=(own...  6.08 us
    all_to_all x1, starting transfers between devices, on_device(): lax.all_to_all(slot_grads, 'dom', split_axis=0, concat_axis=0, tiled=True)  5.27 us
    dot_general x4, matrix products, project(): lax.dot_general(p, w, NT, preferred_element_type=jnp.float32)  4.28 us
  transfers between devices with their start and end apart: 7, of which 5 were waited for; matrix products, arithmetic and copies ran while one was open for 7% of the time, Pallas kernels for 12%

profile of v6, /device:TPU:0, one launch (start us, length us, event | category | flops | bytes accessed | tf_op | source)
XLA Modules:
  0.0 190.1 jit_solution(16412650975762999983)
XLA Ops:
  7.2 0.9 and_select_fusion.2
  8.1 0.8 select_reduce_fusion
  8.9 2.2 %multiply_add_fusion = s32[2,4096]{1,0:T(2,128)S(1)} fusion(s32[2,4096]{1,0:T(2,128)S(1)} %select_reduce_fusion, s32[2,4096]{1,0:T(2,128)} %param.13), kind=kLoop, calls=%fused_computation.35 | loop fusion | flops 253952 | bytes 98304 | tf_op jit(solution)/shard_map/add | solution.py:21
  11.1 0.9 fusion.19
  12.0 1.2 copy-done.3
  13.2 1.6 copy-done.5
  14.8 22.3 %shard_map.96 = (bf16[2048,512]{1,0:T(8,128)(2,1)S(1)}, f32[512,512]{1,0:T(8,128)}) custom-call(s32[1,4096]{1,0:T(1,128)S(1)} %get-tuple-element.19.dst_ref, s32[1,4096]{1,0:T(1,128)S(1)} %get-tuple-element.14.slot_ref, bf16[1024,512]{1,0:T(8,128)(2,1)S(1)} %copy-done.3, bf16[2048,512]{1,0:T(8,128)(2,1)S(1)} %copy-done.5), custom_call_target="tpu_custom_call" | custom-call | flops 12884901888 | bytes 6291456 | tf_op jit(solution)/shard_map/pallas_call | solution.py:78
  37.2 1.3 copy-done.1
  38.6 1.6 copy-done.6
  40.2 22.4 %shard_map.95 = (bf16[2048,512]{1,0:T(8,128)(2,1)S(1)}, f32[512,512]{1,0:T(8,128)}) custom-call(s32[1,4096]{1,0:T(1,128)S(1)} %get-tuple-element.18.dst_ref, s32[1,4096]{1,0:T(1,128)S(1)} %get-tuple-element.15.slot_ref, bf16[1024,512]{1,0:T(8,128)(2,1)S(1)} %copy-done.4, bf16[2048,512]{1,0:T(8,128)(2,1)S(1)} %copy-done.6), custom_call_target="tpu_custom_call" | custom-call | flops 12884901888 | bytes 6291456 | tf_op jit(solution)/shard_map/pallas_call | solution.py:78
  62.6 1.3 dynamic-slice_bitcast_fusion.2
  64.7 0.8 copy-done.2
  65.5 2.1 %convolution_add_fusion = f32[2048,256]{1,0:T(8,128)} fusion(f32[2048,256]{1,0:T(8,128)S(1)} %fusion.3, bf16[2048,512]{1,0:T(8,128)(2,1)S(1)} %copy-done.2, bf16[2,128,512]{2,1,0:T(8,128)(2,1)S(1)} %get-tuple-element.11, bf16[2,128,512]{2,1,0:T(8,128)(2,1)S(1)} %get-tuple-element.12), kind=kOutput, calls=%fused_computation | convolution fusion | flops 537919488 | bytes 6815744 | tf_op jit(solution)/shard_map/dot_general | solution.py:117
  69.7 2.5 %collective-permute-done = f32[2048,256]{1,0:T(8,128)} collective-permute-done((f32[2048,256]{1,0:T(8,128)}, f32[2048,256]{1,0:T(8,128)}, u32[]{:S(2)}, u32[]{:S(2)}) %collective-permute-start) | collective-permute-done | bytes 2097184 | tf_op jit(solution)/shard_map/ppermute | solution.py:141
  72.2 2.3 %slice_add_fusion = f32[2048,128]{1,0:T(8,128)} fusion(f32[2048,256]{1,0:T(8,128)} %collective-permute-done, f32[2048,256]{1,0:T(8,128)S(1)} %convolution_add_fusion.1), kind=kLoop, calls=%fused_computation.3 | loop fusion | flops 262144 | bytes 3145728 | tf_op jit(solution)/shard_map/add | solution.py:144
  74.5 2.8 %collective-permute-start.1 = (f32[2048,128]{1,0:T(8,128)}, f32[2048,128]{1,0:T(8,128)}, u32[]{:S(2)}, u32[]{:S(2)}) collective-permute-start(f32[2048,128]{1,0:T(8,128)} %slice_add_fusion), channel_id=1, source_target_pairs={{0,2},{1,3},{2,0},{3,1},{4,6},{5,7},{6,4},{7,5},{8,10},{9,11},{10,... | collective-permute-start | bytes 3145736 | tf_op jit(solution)/shard_map/ppermute | solution.py:145
  77.3 20.0 %reduce-scatter.3.cloned.1.call-done = f32[128,512]{1,0:T(8,128)} async-done(((f32[512,512]{1,0:T(8,128)}), f32[128,512]{1,0:T(8,128)}) %reduce-scatter.3.cloned.1.call-update) | async-done | bytes 262160 | tf_op jit(solution)/shard_map/reduce_scatter | solution.py:111
  97.4 3.7 %collective-permute-done.1 = f32[2048,128]{1,0:T(8,128)} collective-permute-done((f32[2048,128]{1,0:T(8,128)}, f32[2048,128]{1,0:T(8,128)}, u32[]{:S(2)}, u32[]{:S(2)}) %collective-permute-start.1) | collective-permute-done | bytes 1048608 | tf_op jit(solution)/shard_map/ppermute | solution.py:145
  101.1 2.6 %fusion = f32[2048,128]{1,0:T(8,128)} fusion(f32[2048,128]{1,0:T(8,128)} %collective-permute-done.1, f32[2048,256]{1,0:T(8,128)} %collective-permute-done, f32[2048,256]{1,0:T(8,128)S(1)} %convolution_add_fusion.1), kind=kLoop, calls=%fused_computation.5 | loop fusion | flops 524288 | bytes 4194304 | tf_op jit(solution)/shard_map/add | solution.py:146
  103.8 5.3 %all-to-all-start = ((f32[4,512,128]{2,1,0:T(8,128)}), f32[4,512,128]{2,1,0:T(8,128)S(1)}, u32[]{:S(2)}, u32[]{:S(2)}) async-start(f32[4,512,128]{2,1,0:T(8,128)} %bitcast.37), calls=%async_computation | async-start | bytes 2097152 | tf_op jit(solution)/shard_map/all_to_all | solution.py:205
  109.5 35.2 %all-gather.5.cloned.1.call-done = f32[512,512]{1,0:T(8,128)} async-done(((f32[512,128]{1,0:T(8,128)}), f32[512,512]{1,0:T(8,128)}) %all-gather.5.cloned.1.call-update) | async-done | bytes 1048592 | tf_op jit(solution)/shard_map/all_gather | solution.py:112
  144.7 29.8 %all-gather.3.cloned.1.call-done = f32[512,512]{1,0:T(8,128)} async-done(((f32[128,512]{1,0:T(8,128)}), f32[512,512]{1,0:T(8,128)}) %all-gather.3.cloned.1.call-update) | async-done | bytes 1048592 | tf_op jit(solution)/shard_map/all_gather | solution.py:112
  174.5 3.0 %pad_maximum_fusion = f32[2,512,512]{2,1,0:T(8,128)} fusion(f32[1,512,512]{2,1,0:T(8,128)} %bitcast.39, f32[1,512,512]{2,1,0:T(8,128)} %bitcast.40), kind=kLoop, calls=%fused_computation.2 | loop fusion | flops 524288 | bytes 4194304 | tf_op jit(solution)/shard_map/stack | solution.py:208
  177.5 6.1 %shard_map.97 = f32[2048,128]{1,0:T(8,128)} custom-call(s32[1,2048]{1,0:T(1,128)S(1)} %bitcast.36, f32[2048,128]{1,0:T(8,128)S(1)} %bitcast.35, f32[1024,128]{1,0:T(8,128)S(1)} %fusion.21.refs_2_), custom_call_target="tpu_custom_call" | custom-call | flops 3221225472 | bytes 2097152 | tf_op jit(solution)/shard_map/pallas_call | solution.py:171
  (27 shorter events, 3.4 us)
Async XLA Ops:
  7.2 101.9 %copy-start = (bf16[128,512]{1,0:T(8,128)(2,1)S(1)}, bf16[128,512]{1,0:T(8,128)(2,1)}, u32[]{:S(2)}) copy-start(bf16[128,512]{1,0:T(8,128)(2,1)} %param.11) | copy-start | bytes 393220
  7.2 62.4 %reduce-scatter.5.cloned.1.call-start = ((), (), s32[]{:S(2)}) async-start(), calls=%async_computation.5 | async-start | bytes 1310720 | tf_op jit(solution)/shard_map/reduce_scatter | solution.py:111
  12.0 1.2 copy-start.3
  13.2 1.6 copy-start.5
  14.8 23.7 %copy-start.4 = (bf16[1024,512]{1,0:T(8,128)(2,1)S(1)}, bf16[1024,512]{1,0:T(8,128)(2,1)}, u32[]{:S(2)}) copy-start(bf16[1024,512]{1,0:T(8,128)(2,1)} %grad_ref.3) | copy-start | bytes 3145732
  37.2 1.3 copy-start.1
  38.5 58.8 %reduce-scatter.3.cloned.1.call-start = ((), (), s32[]{:S(2)}) async-start(), calls=%async_computation.3 | async-start | bytes 1310720 | tf_op jit(solution)/shard_map/reduce_scatter | solution.py:111
  38.6 1.6 copy-start.6
  62.6 82.1 %all-gather.5.cloned.1.call-start = ((), (), s32[]{:S(2)}) async-start(), calls=%async_computation.6 | async-start | bytes 1310720 | tf_op jit(solution)/shard_map/all_gather | solution.py:112
  63.9 1.6 copy-start.2
  67.6 4.6 %collective-permute-start = (f32[2048,256]{1,0:T(8,128)}, f32[2048,256]{1,0:T(8,128)}, u32[]{:S(2)}, u32[]{:S(2)}) collective-permute-start(f32[2048,256]{1,0:T(8,128)} %convolution_add_fusion), channel_id=1, source_target_pairs={{0,1},{1,0},{2,3},{3,2},{4,5},{5,4},{6,7},{7,6},{8,9},{9,8},{10,11... | collective-permute-start | bytes 6291464 | tf_op jit(solution)/shard_map/ppermute | solution.py:141
  69.6 104.9 %all-gather.3.cloned.1.call-start = ((), (), s32[]{:S(2)}) async-start(), calls=%async_computation.4 | async-start | bytes 1310720 | tf_op jit(solution)/shard_map/all_gather | solution.py:112
  74.5 26.6 %collective-permute-start.1 = (f32[2048,128]{1,0:T(8,128)}, f32[2048,128]{1,0:T(8,128)}, u32[]{:S(2)}, u32[]{:S(2)}) collective-permute-start(f32[2048,128]{1,0:T(8,128)} %slice_add_fusion), channel_id=1, source_target_pairs={{0,2},{1,3},{2,0},{3,1},{4,6},{5,7},{6,4},{7,5},{8,10},{9,11},{10,... | collective-permute-start | bytes 3145736 | tf_op jit(solution)/shard_map/ppermute | solution.py:145
  103.8 5.3 %copy-start.7 = (s32[4,512]{1,0:T(4,128)S(1)}, s32[4,512]{1,0:T(4,128)}, u32[]{:S(2)}) copy-start(s32[4,512]{1,0:T(4,128)} %param.15) | copy-start | bytes 24580
  103.8 73.8 %all-to-all-start = ((f32[4,512,128]{2,1,0:T(8,128)}), f32[4,512,128]{2,1,0:T(8,128)S(1)}, u32[]{:S(2)}, u32[]{:S(2)}) async-start(f32[4,512,128]{2,1,0:T(8,128)} %bitcast.37), calls=%async_computation | async-start | bytes 2097152 | tf_op jit(solution)/shard_map/all_to_all | solution.py:205
Sparse Core Ops, SparseCore 0:
  38.6 29.8 reduce-scatter.4
  71.5 25.7 reduce-scatter.2
  98.9 45.7 all-gather.4
  146.1 28.3 all-gather.2
